TPU v7x, 32 devices: a whole 2x2x4 slice. The times are simulated.
32 devices in a mesh: section: 2 (over x), col: 16 (over z, y, core).
Axes of the slice: x: 2, y: 2, z: 4, core: 2. Of those that a mesh axis runs over, the one named last changes fastest.
Arguments:
- rhs: float32 [16, 16384], P(None, ('section', 'col')), may hold values from -6 to 6
- inverse_blocks: float32 [128, 128, 128], P(('section', 'col')), may hold values from -1 to 1
- couplings: float32 [128, 2, 128, 128], P(('section', 'col')), may hold values from -0.25 to 0.25
- targets: int32 [128, 2], P(('section', 'col')), may hold values from 0 to 63, as said below
Outputs:
- forward_values: float32 [16, 16384], P(None, ('section', 'col'))
- solution: float32 [16, 16384], P(None, ('section', 'col'))
Inputs may be any that keep to these rules, and one draw needn't show every extreme that they name: The value v = targets[j, k] names the block row with owner column v // 4 and local row v % 4 in the next section group; the 8 values in the rows of one device name 8 different owner columns. Rows of the last section group are not used.
All inputs are finite; a program needn't handle non-finite values.
Results may differ from a plain program's by a relative error of at most 0.0001.
Values sent between devices are 32-bit elements; how exact they have to be, the bound alone decides.
No kernel may reach another device: no remote copies, remote signals or barrier semaphores. Data moves between devices by JAX's collectives and lax.ppermute only.
A program may use at most 64 MiB of HBM per device.

v0:
```python
import jax
import jax.numpy as jnp
from jax import lax
from jax.sharding import PartitionSpec as P

PANELS = 2


precise = lax.Precision.HIGHEST


def passed_along(value, axis, steps):
    count = lax.axis_size(axis)
    first, last = (max(0, -steps), min(count, count - steps))
    return lax.ppermute(value, axis, [(source, source + steps) for source in range(first, last)])


def body(rhs, inverse_blocks, couplings, targets):
    sections = lax.axis_size("section")
    columns = lax.axis_size("col")
    my_section = lax.axis_index("section")
    local_count = inverse_blocks.shape[0]
    block_width = inverse_blocks.shape[1]
    fanout = couplings.shape[1]
    rhs_count = rhs.shape[0]
    groups = PANELS
    group_rhs = rhs_count // groups
    blocks = rhs.reshape(groups, group_rhs, local_count, block_width).transpose(0, 2, 1, 3)
    owners_flat = (targets // local_count).reshape(-1)
    local_rows = (targets % local_count).reshape(-1)
    owner_match = owners_flat[None, :] == jnp.arange(columns, dtype=jnp.int32)[:, None]
    owner_table = owner_match.astype(jnp.float32)
    wanted = jnp.where(
        jnp.any(owner_match, 1),
        jnp.sum(jnp.where(owner_match, local_rows[None, :], 0), 1),
        local_count,
    )
    granted = lax.all_to_all(wanted, "col", split_axis=0, concat_axis=0, tiled=True)
    row_table = (granted[None, :] == jnp.arange(local_count, dtype=jnp.int32)[:, None]).astype(
        jnp.float32
    )

    def forward_step(panel_index, active, state_now, send):
        values, incoming = state_now
        clipped = jnp.clip(panel_index, 0, groups - 1)
        source = lax.dynamic_index_in_dim(blocks, clipped, 0, keepdims=False)
        solved = jnp.einsum("lrb,lbc->lrc", source - incoming, inverse_blocks, precision=precise)
        updated = lax.dynamic_update_index_in_dim(values, solved, clipped, 0)
        values = jnp.where(active, updated, values)
        if send:
            products = jnp.einsum("lrb,lkbc->lkrc", solved, couplings, precision=precise)
            products = products.reshape(local_count * fanout, group_rhs * block_width)
            outgoing = jnp.dot(owner_table, products, precision=precise).reshape(
                columns, group_rhs, block_width
            )
            arrived = lax.all_to_all(outgoing, "col", split_axis=0, concat_axis=0, tiled=True)
            summed = jnp.dot(
                row_table, arrived.reshape(columns, group_rhs * block_width), precision=precise
            )
            summed = summed.reshape(local_count, group_rhs, block_width)
            incoming = passed_along(summed, "section", 1)
        return (values, incoming)

    def backward_step(forward_panels, panel_index, active, state_now, send):
        values, incoming = state_now
        clipped = jnp.clip(panel_index, 0, groups - 1)
        source = lax.dynamic_index_in_dim(forward_panels, clipped, 0, keepdims=False)
        solved = jnp.einsum("lrb,lcb->lrc", source - incoming, inverse_blocks, precision=precise)
        updated = lax.dynamic_update_index_in_dim(values, solved, clipped, 0)
        values = jnp.where(active, updated, values)
        if send:
            lowered = passed_along(solved, "section", -1)
            answers = jnp.dot(
                row_table.T,
                lowered.reshape(local_count, group_rhs * block_width),
                precision=precise,
            )
            answers = answers.reshape(columns, group_rhs, block_width)
            arrived = lax.all_to_all(answers, "col", split_axis=0, concat_axis=0, tiled=True)
            picked = jnp.dot(
                owner_table.T, arrived.reshape(columns, group_rhs * block_width), precision=precise
            )
            picked = picked.reshape(local_count, fanout, group_rhs, block_width)
            incoming = jnp.einsum("lkrc,lkbc->lrb", picked, couplings, precision=precise)
        return (values, incoming)

    empty_state = (
        jnp.zeros((groups, local_count, group_rhs, block_width), jnp.float32),
        jnp.zeros((local_count, group_rhs, block_width), jnp.float32),
    )

    def forward_wave(step_index, state_now):
        panel_index = step_index - my_section
        active = jnp.logical_and(panel_index >= 0, panel_index < groups)
        return forward_step(panel_index, active, state_now, True)

    last_step = sections + groups - 2
    state_now = lax.fori_loop(0, last_step, forward_wave, empty_state)
    final_panel = last_step - my_section
    state_now = forward_step(
        final_panel, jnp.logical_and(final_panel >= 0, final_panel < groups), state_now, False
    )
    forward_panels = state_now[0]

    def backward_wave(step_index, state_now):
        panel_index = step_index - (sections - 1 - my_section)
        active = jnp.logical_and(panel_index >= 0, panel_index < groups)
        return backward_step(forward_panels, panel_index, active, state_now, True)

    state_now = lax.fori_loop(0, last_step, backward_wave, empty_state)
    final_panel = last_step - (sections - 1 - my_section)
    state_now = backward_step(
        forward_panels,
        final_panel,
        jnp.logical_and(final_panel >= 0, final_panel < groups),
        state_now,
        False,
    )
    solved_panels = state_now[0]
    forward_values = forward_panels.transpose(0, 2, 1, 3).reshape(
        rhs_count, local_count * block_width
    )
    solution = solved_panels.transpose(0, 2, 1, 3).reshape(rhs_count, local_count * block_width)
    return (forward_values, solution)


def solution(mesh):
    return jax.shard_map(
        body,
        mesh=mesh,
        in_specs=(
            P(None, ("section", "col")),
            P(("section", "col"), None, None),
            P(("section", "col"), None, None, None),
            P(("section", "col"), None),
        ),
        out_specs=(P(None, ("section", "col")), P(None, ("section", "col"))),
        check_vma=False,
    )
```

profile of v0, /device:TPU:0, one launch (start us, length us, event | category | flops | bytes accessed | tf_op | source)
XLA Modules:
  0.0 91.4 jit_solution(9217044264428204339)
XLA Ops:
  0.7 0.7 copy-done.5
  1.3 0.1 copy.16
  1.5 0.1 fusion.40
  1.6 0.1 copy.17
  1.7 0.1 broadcast_in_dim.52
  1.8 0.1 select_reduce_fusion
  1.9 0.7 copy.18
  2.6 7.4 %all-to-all-start.2 = ((s32[16,1,1]{2,1,0:T(1,128)}), s32[16,1,1]{2,1,0:T(1,128)S(1)}, u32[]{:S(2)}, u32[]{:S(2)}) async-start(s32[16,1,1]{2,1,0:T(1,128)} %copy.18), calls=%async_computation.2 | async-start | bytes 16384 | tf_op jit(solution)/shard_map/all_to_all | solution.py:38
  10.0 6.3 %all-to-all-done.2 = s32[16,1,1]{2,1,0:T(1,128)S(1)} async-done(((s32[16,1,1]{2,1,0:T(1,128)}), s32[16,1,1]{2,1,0:T(1,128)S(1)}, u32[]{:S(2)}, u32[]{:S(2)}) %all-to-all-start.2) | async-done | bytes 96 | tf_op jit(solution)/shard_map/all_to_all | solution.py:38
  16.3 0.4 reduce
  16.7 35.6 %while.34 = (s32[]{:T(128)}, f32[2,4,8,128]{3,2,1,0:T(8,128)S(1)}, f32[4,8,128]{2,1,0:T(8,128)S(1)}, s32[]{:T(128)}, f32[2,4,8,128]{3,2,1,0:T(8,128)S(1)}, /*ind...) while((s32[]{:T(128)}, f32[2,4,8,128]{3,2,1,0:T(8,128)S(1)}, ...), condition=%wide.region_3.4_spmd.clone, body=%wide.region_2.3_spmd.clone.sunk | while | flops 21242248 | bytes 1460022 | solution.py:98
  16.7 1.3 %fusion.74 = (f32[2,4,8,128]{3,2,1,0:T(8,128)S(1)}, f32[4,8,128]{2,1,0:T(8,128)S(1)}) fusion(f32[2,4,8,128]{3,2,1,0:T(8,128)S(1)} %get-tuple-element.593, s32[]{:T(128)S(6)} %min.29, pred[]{:T(512)S(6)} %and.43, f32[4,128,128]{2,1,0:T(8,128)} %get-tuple-element.609, f32[4,8,128]{2,1,0:T(8,128)S(1)} %get-tuple-element.594, ...), kind=kOutput, calls=%fused_computation.14.clone.1 | convolution fusion | flops 6299648 | bytes 345600 | tf_op jit(solution)/shard_map/while/body/eval_jaxpr/lrb,lbc->lrc/dot_general | solution.py:47
  18.0 1.4 %fusion.75 = f32[4,8,2,128]{3,1,2,0:T(8,128)S(1)} fusion(f32[4,2,128,128]{3,2,1,0:T(8,128)} %get-tuple-element.610, f32[4,8,128]{2,1,0:T(8,128)S(1)} %get-tuple-element.568), kind=kOutput, calls=%fused_computation.11.clone.1 | convolution fusion | flops 12582912 | bytes 573440 | tf_op jit(solution)/shard_map/while/body/eval_jaxpr/lrb,lkbc->lkrc/dot_general | solution.py:51
  19.4 0.2 convolution_bitcast_fusion.12
  19.6 9.5 %all_to_all.30 = f32[16,8,128]{2,1,0:T(8,128)S(1)} all-to-all(f32[16,8,128]{2,1,0:T(8,128)S(1)} %bitcast.156), channel_id=1, replica_groups=mesh['section'=2,'col'=16] {'col'}, dimensions={0} | all-to-all | bytes 131072 | tf_op jit(solution)/shard_map/while/body/eval_jaxpr/all_to_all | solution.py:56
  29.1 0.2 convolution_bitcast_fusion.13
  29.3 3.4 %collective-permute-start = (f32[4,8,128]{2,1,0:T(8,128)S(1)}, f32[4,8,128]{2,1,0:T(8,128)S(1)}, u32[]{:S(2)}, u32[]{:S(2)}) collective-permute-start(f32[4,8,128]{2,1,0:T(8,128)S(1)} %bitcast.163), channel_id=1, source_target_pairs={{0,16},{1,17},{2,18},{3,19},{4,20},{5,21},{6,22},{7,23},{8,24},{9,... | collective-permute-start | bytes 49160 | tf_op jit(solution)/shard_map/while/body/eval_jaxpr/ppermute | solution.py:15
  32.7 1.4 %collective-permute-done = f32[4,8,128]{2,1,0:T(8,128)S(1)} collective-permute-done((f32[4,8,128]{2,1,0:T(8,128)S(1)}, f32[4,8,128]{2,1,0:T(8,128)S(1)}, u32[]{:S(2)}, u32[]{:S(2)}) %collective-permute-start) | collective-permute-done | bytes 16416 | tf_op jit(solution)/shard_map/while/body/eval_jaxpr/ppermute | solution.py:15
  34.1 1.3 %fusion.74 = (f32[2,4,8,128]{3,2,1,0:T(8,128)S(1)}, f32[4,8,128]{2,1,0:T(8,128)S(1)}) fusion(f32[2,4,8,128]{3,2,1,0:T(8,128)S(1)} %get-tuple-element.593, s32[]{:T(128)S(6)} %min.29, pred[]{:T(512)S(6)} %and.43, f32[4,128,128]{2,1,0:T(8,128)} %get-tuple-element.609, f32[4,8,128]{2,1,0:T(8,128)S(1)} %get-tuple-element.594, ...), kind=kOutput, calls=%fused_computation.14.clone.1 | convolution fusion | flops 6299648 | bytes 345600 | tf_op jit(solution)/shard_map/while/body/eval_jaxpr/lrb,lbc->lrc/dot_general | solution.py:47
  35.4 1.4 %fusion.75 = f32[4,8,2,128]{3,1,2,0:T(8,128)S(1)} fusion(f32[4,2,128,128]{3,2,1,0:T(8,128)} %get-tuple-element.610, f32[4,8,128]{2,1,0:T(8,128)S(1)} %get-tuple-element.568), kind=kOutput, calls=%fused_computation.11.clone.1 | convolution fusion | flops 12582912 | bytes 573440 | tf_op jit(solution)/shard_map/while/body/eval_jaxpr/lrb,lkbc->lkrc/dot_general | solution.py:51
  36.8 0.2 convolution_bitcast_fusion.12
  37.0 9.5 %all_to_all.30 = f32[16,8,128]{2,1,0:T(8,128)S(1)} all-to-all(f32[16,8,128]{2,1,0:T(8,128)S(1)} %bitcast.156), channel_id=1, replica_groups=mesh['section'=2,'col'=16] {'col'}, dimensions={0} | all-to-all | bytes 131072 | tf_op jit(solution)/shard_map/while/body/eval_jaxpr/all_to_all | solution.py:56
  46.5 0.2 convolution_bitcast_fusion.13
  46.7 4.2 %collective-permute-start = (f32[4,8,128]{2,1,0:T(8,128)S(1)}, f32[4,8,128]{2,1,0:T(8,128)S(1)}, u32[]{:S(2)}, u32[]{:S(2)}) collective-permute-start(f32[4,8,128]{2,1,0:T(8,128)S(1)} %bitcast.163), channel_id=1, source_target_pairs={{0,16},{1,17},{2,18},{3,19},{4,20},{5,21},{6,22},{7,23},{8,24},{9,... | collective-permute-start | bytes 49160 | tf_op jit(solution)/shard_map/while/body/eval_jaxpr/ppermute | solution.py:15
  50.9 1.4 %collective-permute-done = f32[4,8,128]{2,1,0:T(8,128)S(1)} collective-permute-done((f32[4,8,128]{2,1,0:T(8,128)S(1)}, f32[4,8,128]{2,1,0:T(8,128)S(1)}, u32[]{:S(2)}, u32[]{:S(2)}) %collective-permute-start) | collective-permute-done | bytes 16416 | tf_op jit(solution)/shard_map/while/body/eval_jaxpr/ppermute | solution.py:15
  52.3 1.3 %fusion.37 = f32[2,4,8,128]{3,2,1,0:T(8,128)S(1)} fusion(f32[2,4,8,128]{3,2,1,0:T(8,128)S(1)} %get-tuple-element.370, s32[]{:T(128)S(6)} %min.23, f32[4,128,128]{2,1,0:T(8,128)} %get-tuple-element.653, f32[4,8,128]{2,1,0:T(8,128)S(1)} %get-tuple-element.371, f32[2,8,4,128]{3,1,2,0:T(8,128)S(1)} %bitcast.165, pred[]{:T(512)S(6)} %and.35), kind=kOutput, calls=%fused_computation.49 | convolution fusion | flops 6299648 | bytes 329216 | tf_op jit(solution)/shard_map/lrb,lbc->lrc/dot_general | solution.py:47
  53.7 36.4 %while.35 = (s32[]{:T(128)}, f32[2,4,8,128]{3,2,1,0:T(8,128)S(1)}, f32[4,8,128]{2,1,0:T(8,128)S(1)}, s32[]{:T(128)}, f32[2,4,8,128]{3,2,1,0:T(8,128)S(1)}, /*ind...) while((s32[]{:T(128)}, f32[2,4,8,128]{3,2,1,0:T(8,128)S(1)}, ...), condition=%wide.region_5.6_spmd.clone, body=%wide.region_4.5_spmd.clone.sunk | while | flops 21242248 | bytes 3655538 | solution.py:110
  53.7 0.5 fusion.83
  54.2 1.3 %collective-permute-start.1 = (f32[4,8,128]{2,1,0:T(8,128)S(1)}, f32[4,8,128]{2,1,0:T(8,128)S(1)}, u32[]{:S(2)}, u32[]{:S(2)}) collective-permute-start(f32[4,8,128]{2,1,0:T(8,128)S(1)} %get-tuple-element.579), channel_id=1, source_target_pairs={{16,0},{17,1},{18,2},{19,3},{20,4},{21,5},{22,6},{23,7},{24,8},{25... | collective-permute-start | bytes 49160 | tf_op jit(solution)/shard_map/while/body/eval_jaxpr/ppermute | solution.py:15
  55.5 4.3 %collective-permute-done.1 = f32[4,8,128]{2,1,0:T(8,128)S(1)} collective-permute-done((f32[4,8,128]{2,1,0:T(8,128)S(1)}, f32[4,8,128]{2,1,0:T(8,128)S(1)}, u32[]{:S(2)}, u32[]{:S(2)}) %collective-permute-start.1) | collective-permute-done | bytes 16416 | tf_op jit(solution)/shard_map/while/body/eval_jaxpr/ppermute | solution.py:15
  59.9 0.3 convolution_bitcast_fusion.14
  60.1 0.6 copy.61
  60.8 3.5 %all-to-all-start.1 = ((f32[16,8,128]{2,1,0:T(8,128)}), f32[16,8,128]{2,1,0:T(8,128)S(1)}, u32[]{:S(2)}, u32[]{:S(2)}) async-start(f32[16,8,128]{2,1,0:T(8,128)} %bitcast.152), calls=%async_computation.1 | async-start | bytes 131072 | tf_op jit(solution)/shard_map/while/body/eval_jaxpr/all_to_all | solution.py:79
  64.3 6.9 %all-to-all-done.1 = f32[16,8,128]{2,1,0:T(8,128)S(1)} async-done(((f32[16,8,128]{2,1,0:T(8,128)}), f32[16,8,128]{2,1,0:T(8,128)S(1)}, u32[]{:S(2)}, u32[]{:S(2)}) %all-to-all-start.1) | async-done | bytes 65568 | tf_op jit(solution)/shard_map/while/body/eval_jaxpr/all_to_all | solution.py:79
  71.1 0.2 convolution_bitcast_fusion.15
  71.4 0.5 convolution_bitcast_fusion.16
  71.9 0.5 fusion.83
  72.4 1.3 %collective-permute-start.1 = (f32[4,8,128]{2,1,0:T(8,128)S(1)}, f32[4,8,128]{2,1,0:T(8,128)S(1)}, u32[]{:S(2)}, u32[]{:S(2)}) collective-permute-start(f32[4,8,128]{2,1,0:T(8,128)S(1)} %get-tuple-element.579), channel_id=1, source_target_pairs={{16,0},{17,1},{18,2},{19,3},{20,4},{21,5},{22,6},{23,7},{24,8},{25... | collective-permute-start | bytes 49160 | tf_op jit(solution)/shard_map/while/body/eval_jaxpr/ppermute | solution.py:15
  73.7 4.3 %collective-permute-done.1 = f32[4,8,128]{2,1,0:T(8,128)S(1)} collective-permute-done((f32[4,8,128]{2,1,0:T(8,128)S(1)}, f32[4,8,128]{2,1,0:T(8,128)S(1)}, u32[]{:S(2)}, u32[]{:S(2)}) %collective-permute-start.1) | collective-permute-done | bytes 16416 | tf_op jit(solution)/shard_map/while/body/eval_jaxpr/ppermute | solution.py:15
  78.1 0.3 convolution_bitcast_fusion.14
  78.3 0.6 copy.61
  79.0 3.5 %all-to-all-start.1 = ((f32[16,8,128]{2,1,0:T(8,128)}), f32[16,8,128]{2,1,0:T(8,128)S(1)}, u32[]{:S(2)}, u32[]{:S(2)}) async-start(f32[16,8,128]{2,1,0:T(8,128)} %bitcast.152), calls=%async_computation.1 | async-start | bytes 131072 | tf_op jit(solution)/shard_map/while/body/eval_jaxpr/all_to_all | solution.py:79
  82.5 6.9 %all-to-all-done.1 = f32[16,8,128]{2,1,0:T(8,128)S(1)} async-done(((f32[16,8,128]{2,1,0:T(8,128)}), f32[16,8,128]{2,1,0:T(8,128)S(1)}, u32[]{:S(2)}, u32[]{:S(2)}) %all-to-all-start.1) | async-done | bytes 65568 | tf_op jit(solution)/shard_map/while/body/eval_jaxpr/all_to_all | solution.py:79
  89.3 0.2 convolution_bitcast_fusion.15
  89.6 0.5 convolution_bitcast_fusion.16
  90.1 0.5 fusion.35
  90.6 0.1 copy-done.2
  90.7 0.6 copy-done.3
  (24 shorter events, 0.2 us)
Async XLA Ops:
  0.6 0.7 copy-start.5
  2.6 13.7 %all-to-all-start.2 = ((s32[16,1,1]{2,1,0:T(1,128)}), s32[16,1,1]{2,1,0:T(1,128)S(1)}, u32[]{:S(2)}, u32[]{:S(2)}) async-start(s32[16,1,1]{2,1,0:T(1,128)} %copy.18), calls=%async_computation.2 | async-start | bytes 16384 | tf_op jit(solution)/shard_map/all_to_all | solution.py:38
  10.0 6.7 %copy-start.4 = (f32[16,512]{1,0:T(8,128)S(1)}, f32[16,512]{1,0:T(8,128)}, u32[]{:S(2)}) copy-start(f32[16,512]{1,0:T(8,128)} %param.8) | copy-start | bytes 98308
  29.3 4.8 %collective-permute-start = (f32[4,8,128]{2,1,0:T(8,128)S(1)}, f32[4,8,128]{2,1,0:T(8,128)S(1)}, u32[]{:S(2)}, u32[]{:S(2)}) collective-permute-start(f32[4,8,128]{2,1,0:T(8,128)S(1)} %bitcast.163), channel_id=1, source_target_pairs={{0,16},{1,17},{2,18},{3,19},{4,20},{5,21},{6,22},{7,23},{8,24},{9,... | collective-permute-start | bytes 49160 | tf_op jit(solution)/shard_map/while/body/eval_jaxpr/ppermute | solution.py:15
  46.7 5.6 %collective-permute-start = (f32[4,8,128]{2,1,0:T(8,128)S(1)}, f32[4,8,128]{2,1,0:T(8,128)S(1)}, u32[]{:S(2)}, u32[]{:S(2)}) collective-permute-start(f32[4,8,128]{2,1,0:T(8,128)S(1)} %bitcast.163), channel_id=1, source_target_pairs={{0,16},{1,17},{2,18},{3,19},{4,20},{5,21},{6,22},{7,23},{8,24},{9,... | collective-permute-start | bytes 49160 | tf_op jit(solution)/shard_map/while/body/eval_jaxpr/ppermute | solution.py:15
  52.3 1.4 %copy-start.1 = (f32[4,128,128]{2,1,0:T(8,128)S(1)}, f32[4,128,128]{2,1,0:T(8,128)}, u32[]{:S(2)}) copy-start(f32[4,128,128]{2,1,0:T(8,128)} %get-tuple-element.653) | copy-start | bytes 786436
  53.7 17.7 %copy-start = (f32[4,2,128,128]{3,2,1,0:T(8,128)S(1)}, f32[4,2,128,128]{3,2,1,0:T(8,128)}, u32[]{:S(2)}) copy-start(f32[4,2,128,128]{3,2,1,0:T(8,128)} %get-tuple-element.646) | copy-start | bytes 1572868 | tf_op jit(solution)/shard_map/while
  54.2 5.6 %collective-permute-start.1 = (f32[4,8,128]{2,1,0:T(8,128)S(1)}, f32[4,8,128]{2,1,0:T(8,128)S(1)}, u32[]{:S(2)}, u32[]{:S(2)}) collective-permute-start(f32[4,8,128]{2,1,0:T(8,128)S(1)} %get-tuple-element.579), channel_id=1, source_target_pairs={{16,0},{17,1},{18,2},{19,3},{20,4},{21,5},{22,6},{23,7},{24,8},{25... | collective-permute-start | bytes 49160 | tf_op jit(solution)/shard_map/while/body/eval_jaxpr/ppermute | solution.py:15
  60.8 10.4 %all-to-all-start.1 = ((f32[16,8,128]{2,1,0:T(8,128)}), f32[16,8,128]{2,1,0:T(8,128)S(1)}, u32[]{:S(2)}, u32[]{:S(2)}) async-start(f32[16,8,128]{2,1,0:T(8,128)} %bitcast.152), calls=%async_computation.1 | async-start | bytes 131072 | tf_op jit(solution)/shard_map/while/body/eval_jaxpr/all_to_all | solution.py:79
  71.9 17.7 %copy-start = (f32[4,2,128,128]{3,2,1,0:T(8,128)S(1)}, f32[4,2,128,128]{3,2,1,0:T(8,128)}, u32[]{:S(2)}) copy-start(f32[4,2,128,128]{3,2,1,0:T(8,128)} %get-tuple-element.646) | copy-start | bytes 1572868 | tf_op jit(solution)/shard_map/while
  72.4 5.6 %collective-permute-start.1 = (f32[4,8,128]{2,1,0:T(8,128)S(1)}, f32[4,8,128]{2,1,0:T(8,128)S(1)}, u32[]{:S(2)}, u32[]{:S(2)}) collective-permute-start(f32[4,8,128]{2,1,0:T(8,128)S(1)} %get-tuple-element.579), channel_id=1, source_target_pairs={{16,0},{17,1},{18,2},{19,3},{20,4},{21,5},{22,6},{23,7},{24,8},{25... | collective-permute-start | bytes 49160 | tf_op jit(solution)/shard_map/while/body/eval_jaxpr/ppermute | solution.py:15
  79.0 10.4 %all-to-all-start.1 = ((f32[16,8,128]{2,1,0:T(8,128)}), f32[16,8,128]{2,1,0:T(8,128)S(1)}, u32[]{:S(2)}, u32[]{:S(2)}) async-start(f32[16,8,128]{2,1,0:T(8,128)} %bitcast.152), calls=%async_computation.1 | async-start | bytes 131072 | tf_op jit(solution)/shard_map/while/body/eval_jaxpr/all_to_all | solution.py:79
  90.1 0.6 copy-start.2
  90.7 0.6 copy-start.3
where the time goes:
time: 92 us; the launch traced here: 91.4 us
  waiting for transfers between devices  31.5 us (34%)
  starting transfers between devices  24.6 us (27%)
  blocking collectives  19 us (21%)
  matrix products  10.9 us (12%)
  local copies, waits for them, and re-layouts  3.82 us (4%)
    all_to_all x2, blocking collectives, forward_step(): lax.all_to_all(outgoing, 'col', split_axis=0, concat_axis=0, tiled=True)  19 us
    all_to_all x2, waiting for transfers between devices, backward_step(): lax.all_to_all(answers, 'col', split_axis=0, concat_axis=0, tiled=True)  13.7 us
    ppermute x4, waiting for transfers between devices, passed_along(): lax.ppermute(value, axis, [(source, source + steps) for source in range(f...  11.5 us
    ppermute x4, starting transfers between devices, passed_along(): lax.ppermute(value, axis, [(source, source + steps) for source in range(f...  10.2 us
    all_to_all x1, starting transfers between devices, body(): lax.all_to_all(wanted, 'col', split_axis=0, concat_axis=0, tiled=True)  7.39 us
    all_to_all x2, starting transfers between devices, backward_step(): lax.all_to_all(answers, 'col', split_axis=0, concat_axis=0, tiled=True)  7 us
    all_to_all x1, waiting for transfers between devices, body(): lax.all_to_all(wanted, 'col', split_axis=0, concat_axis=0, tiled=True)  6.31 us
    dot_general x3, matrix products, forward_step(): jnp.einsum('lrb,lbc->lrc', source - incoming, inverse_blocks, precision=p...  3.86 us
  transfers between devices with their start and end apart: 7, of which 7 were waited for; matrix products, arithmetic and copies ran while one was open for 0% of the time, Pallas kernels for 0%

commit v1 on v0

v1 whole, which is shorter than its diff:
```python
import functools

import jax
import jax.numpy as jnp
from jax import lax
from jax.experimental import pallas as pl
from jax.experimental.pallas import tpu as pltpu
from jax.sharding import PartitionSpec as P

INDEX_ROWS = 8
VMEM = pl.BlockSpec(memory_space=pltpu.VMEM)
SMEM = pl.BlockSpec(memory_space=pltpu.SMEM)

precise = lax.Precision.HIGHEST


def times(left, right):
    return lax.dot_general(left, right, (((1,), (0,)), ((), ())), precision=precise)


def times_transposed(left, right):
    return lax.dot_general(left, right, (((1,), (1,)), ((), ())), precision=precise)


def kernel_call(kernel, out_shape, specs, name):
    return pl.pallas_call(
        kernel,
        out_shape=out_shape,
        in_specs=specs,
        out_specs=jax.tree.map(lambda _: VMEM, out_shape),
        compiler_params=pltpu.CompilerParams(vmem_limit_bytes=16 * 2**20),
        name=name,
    )


def summed_by_row(arrived_ref, local_count, rhs_count):
    sums = [None] * local_count
    for column in range(arrived_ref.shape[0]):
        block = arrived_ref[column, :rhs_count, :]
        row = arrived_ref[column, rhs_count : rhs_count + 1, :]
        for local in range(local_count):
            term = jnp.where(row == local, block, 0.0)
            sums[local] = term if sums[local] is None else sums[local] + term
    return sums


def place_answers(arrived_ref, answers_ref, solved, rhs_count):
    for column in range(arrived_ref.shape[0]):
        row = arrived_ref[column, rhs_count : rhs_count + 1, :]
        answer = jnp.zeros_like(solved[0])
        for local, values in enumerate(solved):
            answer = jnp.where(row == local, values, answer)
        answers_ref[column] = answer


def forward_kernel(targets_ref, rhs_ref, incoming_ref, inverse_ref, couplings_ref, values_ref, out_ref):
    local_count, width, _ = inverse_ref.shape
    fanout = couplings_ref.shape[1]
    rhs_count = rhs_ref.shape[0]
    out_ref[...] = jnp.full(out_ref.shape, -1.0, jnp.float32)
    for local in range(local_count):
        lanes = slice(local * width, (local + 1) * width)
        source = rhs_ref[:, lanes] - incoming_ref[:, lanes]
        solved = times(source, inverse_ref[local])
        values_ref[:, lanes] = solved
        for k in range(fanout):
            target = targets_ref[local, k]
            owner = target // local_count
            out_ref[owner, :rhs_count, :] = times(solved, couplings_ref[local, k])
            out_ref[owner, rhs_count:, :] = jnp.full(
                (out_ref.shape[1] - rhs_count, width), target % local_count, jnp.int32
            ).astype(jnp.float32)


def sum_kernel(arrived_ref, sums_ref):
    rhs_count, width = sums_ref.shape[0], arrived_ref.shape[2]
    local_count = sums_ref.shape[1] // width
    for local, total in enumerate(summed_by_row(arrived_ref, local_count, rhs_count)):
        sums_ref[:, local * width : (local + 1) * width] = total


def last_kernel(arrived_ref, rhs_ref, inverse_ref, pair_ref, answers_ref):
    local_count, width, _ = inverse_ref.shape
    rhs_count = rhs_ref.shape[0]
    sums = summed_by_row(arrived_ref, local_count, rhs_count)
    solved = []
    for local in range(local_count):
        lanes = slice(local * width, (local + 1) * width)
        forward = times(rhs_ref[:, lanes] - sums[local], inverse_ref[local])
        backward = times_transposed(forward, inverse_ref[local])
        pair_ref[0, :, lanes] = forward
        pair_ref[1, :, lanes] = backward
        solved.append(backward)
    place_answers(arrived_ref, answers_ref, solved, rhs_count)


def place_kernel(arrived_ref, solved_ref, answers_ref):
    rhs_count, width = solved_ref.shape[0], arrived_ref.shape[2]
    local_count = solved_ref.shape[1] // width
    solved = [solved_ref[:, i * width : (i + 1) * width] for i in range(local_count)]
    place_answers(arrived_ref, answers_ref, solved, rhs_count)


def backward_kernel(targets_ref, picked_ref, values_ref, inverse_ref, couplings_ref, solution_ref):
    local_count, width, _ = inverse_ref.shape
    for local in range(local_count):
        lanes = slice(local * width, (local + 1) * width)
        source = values_ref[:, lanes]
        for k in range(couplings_ref.shape[1]):
            owner = targets_ref[local, k] // local_count
            source = source - times_transposed(picked_ref[owner], couplings_ref[local, k])
        solution_ref[:, lanes] = times_transposed(source, inverse_ref[local])


def body(rhs, inverse_blocks, couplings, targets):
    sections = lax.axis_size("section")
    columns = lax.axis_size("col")
    my_section = lax.axis_index("section")
    local_count, width, _ = inverse_blocks.shape
    rhs_count = rhs.shape[0]
    up = [(s, (s + 1) % sections) for s in range(sections)]
    down = [(s, (s - 1) % sections) for s in range(sections)]
    flat = jax.ShapeDtypeStruct(rhs.shape, jnp.float32)
    slots = jax.ShapeDtypeStruct((columns, rhs_count + INDEX_ROWS, width), jnp.float32)
    answered = jax.ShapeDtypeStruct((columns, rhs_count, width), jnp.float32)
    pair = jax.ShapeDtypeStruct((2,) + rhs.shape, jnp.float32)

    def exchanged(value):
        return lax.all_to_all(value, "col", split_axis=0, concat_axis=0, tiled=True)

    next_inverse = lax.ppermute(inverse_blocks, "section", down)
    next_rhs = lax.ppermute(rhs, "section", down)

    incoming = jnp.zeros_like(rhs)
    for step in range(sections - 1):
        values, outgoing = kernel_call(
            forward_kernel, (flat, slots), [SMEM, VMEM, VMEM, VMEM, VMEM], "forward"
        )(targets, rhs, incoming, inverse_blocks, couplings)
        arrived = exchanged(outgoing)
        if step < sections - 2:
            sums = kernel_call(sum_kernel, flat, [VMEM], "sum_rows")(arrived)
            moved = lax.ppermute(sums, "section", up)
            incoming = jnp.where(my_section == 0, 0.0, moved)

    last, answers = kernel_call(last_kernel, (pair, answered), [VMEM, VMEM, VMEM], "last_section")(
        arrived, next_rhs, next_inverse
    )
    for step in range(sections - 1):
        picked = exchanged(answers)
        solved = kernel_call(
            backward_kernel, flat, [SMEM, VMEM, VMEM, VMEM, VMEM], "backward"
        )(targets, picked, values, inverse_blocks, couplings)
        if step < sections - 2:
            moved = lax.ppermute(solved, "section", down)
            following = jnp.where(my_section == sections - 2, last[1], moved)
            answers = kernel_call(place_kernel, answered, [VMEM, VMEM], "place")(arrived, following)

    final = lax.ppermute(last, "section", up)
    is_last = my_section == sections - 1
    return jnp.where(is_last, final[0], values), jnp.where(is_last, final[1], solved)


def solution(mesh):
    return jax.shard_map(
        body,
        mesh=mesh,
        in_specs=(
            P(None, ("section", "col")),
            P(("section", "col"), None, None),
            P(("section", "col"), None, None, None),
            P(("section", "col"), None),
        ),
        out_specs=(P(None, ("section", "col")), P(None, ("section", "col"))),
        check_vma=False,
    )
```

time: 92 us -> 42 us (0.46)
  blocking collectives: 19 us -> 0 us
  waiting for transfers between devices: 31.5 us -> 13.7 us
  matrix products: 10.9 us -> 0 us
  starting transfers between devices: 24.6 us -> 16.9 us
  Pallas kernels: 0 us -> 6.87 us
  local copies, waits for them, and re-layouts: 3.82 us -> 2.77 us
    all_to_all x2 -> x0, blocking collectives: 19 us -> none  [forward_step(): lax.all_to_all(outgoing, 'col', split_axis=0, concat_axis=0, tiled=True)]
    all_to_all x3 -> x2, waiting for transfers between devices: 20 us -> 6.38 us  [exchanged(): return lax.all_to_all(value, 'col', split_axis=0, concat_axis=0, tiled=True)]
    dot_general x18 -> x0, matrix products: 10.9 us -> none  [the longest x3 3.86 us: forward_step(): jnp.einsum('lrb,lbc->lrc', source - incoming, inverse_blocks, precision=p...]
    pallas_call x0 -> x3, Pallas kernels: none -> 6.87 us  [the longest x1 2.61 us: body(): kernel_call(backward_kernel, flat, [SMEM, VMEM, VMEM, VMEM, VMEM], 'backw...]
    ppermute x4 -> x3, starting transfers between devices: 10.2 us -> 3.65 us  [the longest x1 1.56 us: body(): next_inverse = lax.ppermute(inverse_blocks, 'section', down)]
    ppermute x4 -> x3, waiting for transfers between devices: 11.5 us -> 7.32 us  [the longest x1 7.32 us: body(): next_rhs = lax.ppermute(rhs, 'section', down)]
    unnamed x10 -> x11, local copies, waits for them, and re-layouts: 1.4 us -> 2.77 us
    while x12 -> x0, local copies, waits for them, and re-layouts: 1.36 us -> none
  transfers between devices with their start and end apart: 7 -> 5, of which waited for: 7 -> 2; matrix products, arithmetic and copies ran while one was open for 0% -> 0% of each run, Pallas kernels for 0% -> 6%
where the time goes in v1:
time: 42 us; the launch traced here: 41.6 us
  starting transfers between devices  16.9 us (40%)
  waiting for transfers between devices  13.7 us (33%)
  Pallas kernels  6.87 us (16%)
  local copies, waits for them, and re-layouts  2.77 us (7%)
  between operations  0.68 us (2%)
  other arithmetic  0.67 us (2%)
    all_to_all x2, starting transfers between devices, exchanged(): return lax.all_to_all(value, 'col', split_axis=0, concat_axis=0, tiled=True)  13.2 us
    ppermute x1, waiting for transfers between devices, body(): next_rhs = lax.ppermute(rhs, 'section', down)  7.32 us
    all_to_all x2, waiting for transfers between devices, exchanged(): return lax.all_to_all(value, 'col', split_axis=0, concat_axis=0, tiled=True)  6.38 us
    unnamed x11, local copies, waits for them, and re-layouts  2.77 us
    pallas_call x1, Pallas kernels, body(): kernel_call(backward_kernel, flat, [SMEM, VMEM, VMEM, VMEM, VMEM], 'backw...  2.61 us
    pallas_call x1, Pallas kernels, body(): kernel_call(forward_kernel, (flat, slots), [SMEM, VMEM, VMEM, VMEM, VMEM]...  2.58 us
    pallas_call x1, Pallas kernels, body(): kernel_call(last_kernel, (pair, answered), [VMEM, VMEM, VMEM], 'last_sect...  1.68 us
    ppermute x1, starting transfers between devices, body(): next_inverse = lax.ppermute(inverse_blocks, 'section', down)  1.56 us
  transfers between devices with their start and end apart: 5, of which 2 were waited for; matrix products, arithmetic and copies ran while one was open for 0% of the time, Pallas kernels for 6%

profile of v1, /device:TPU:0, one launch (start us, length us, event | category | flops | bytes accessed | tf_op | source)
XLA Modules:
  0.0 41.6 jit_solution(13449316428731520811)
XLA Ops:
  0.6 0.0 copy-start.4
  0.6 0.8 %copy.6.targets_ref = s32[4,2]{1,0:T(4,128)S(1)} copy(s32[4,2]{0,1:T(2,128)} %param.7) | data formatting | bytes 64 | tf_op args[3]
  1.4 0.0 copy-done.4
  1.4 0.0 copy-start
  1.4 1.0 %copy-done = f32[4,2,128,128]{3,2,1,0:T(8,128)S(1)} copy-done((f32[4,2,128,128]{3,2,1,0:T(8,128)S(1)}, f32[4,2,128,128]{3,2,1,0:T(8,128)}, u32[]{:S(2)}) %copy-start) | copy-done | bytes 524312
  2.5 0.0 copy-start.2
  2.5 0.9 %copy-done.2 = f32[4,128,128]{2,1,0:T(8,128)S(1)} copy-done((f32[4,128,128]{2,1,0:T(8,128)S(1)}, f32[4,128,128]{2,1,0:T(8,128)}, u32[]{:S(2)}) %copy-start.2) | copy-done | bytes 262168
  3.4 2.6 %forward.1 = (f32[16,512]{1,0:T(8,128)S(1)}, f32[16,24,128]{2,1,0:T(8,128)}) custom-call(s32[4,2]{1,0:T(4,128)S(1)} %copy.6.targets_ref, f32[16,512]{1,0:T(8,128)S(1)} %copy-done.4, f32[16,512]{1,0:T(8,128)S(1)} %broadcast_in_dim.3.incoming_ref, f32[4,128,128]{2,1,0:T(8,128)S(1)} %copy-done.2, f32[4,2,128,128]{3,2,1,0:T(8,128)S(1)} %copy-done), custom_call_target="tpu_custom_call" | custom-call | tf_op jit(solution)/shard_map/forward/pallas_call | solution.py:136
  6.0 0.0 copy-start.3
  6.0 0.0 copy-start.1
  6.0 7.5 %all-to-all-start = ((f32[16,24,128]{2,1,0:T(8,128)}), f32[16,24,128]{2,1,0:T(8,128)S(1)}, u32[]{:S(2)}, u32[]{:S(2)}) async-start(f32[16,24,128]{2,1,0:T(8,128)} %get-tuple-element.6), calls=%async_computation | async-start | bytes 393216 | tf_op jit(solution)/shard_map/all_to_all | solution.py:129
  13.5 0.0 copy-done.3
  13.5 1.6 %collective-permute-start.1 = (f32[4,128,128]{2,1,0:T(8,128)S(1)}, f32[4,128,128]{2,1,0:T(8,128)S(1)}, u32[]{:S(2)}, u32[]{:S(2)}) collective-permute-start(f32[4,128,128]{2,1,0:T(8,128)S(1)} %copy-done.3), channel_id=1, source_target_pairs={{0,16},{16,0},{1,17},{17,1},{2,18},{18,2},{3,19},{19,3},{4,20},{20... | collective-permute-start | bytes 786440 | tf_op jit(solution)/shard_map/ppermute | solution.py:131
  15.1 0.5 %collective-permute-start = (f32[16,512]{1,0:T(8,128)S(1)}, f32[16,512]{1,0:T(8,128)S(1)}, u32[]{:S(2)}, u32[]{:S(2)}) collective-permute-start(f32[16,512]{1,0:T(8,128)S(1)} %copy-done.4), channel_id=1, source_target_pairs={{0,16},{16,0},{1,17},{17,1},{2,18},{18,2},{3,19},{19,3},{4,20},{20... | collective-permute-start | bytes 98312 | tf_op jit(solution)/shard_map/ppermute | solution.py:132
  15.6 7.3 %collective-permute-done.rhs_ref = f32[16,512]{1,0:T(8,128)S(1)} collective-permute-done((f32[16,512]{1,0:T(8,128)S(1)}, f32[16,512]{1,0:T(8,128)S(1)}, u32[]{:S(2)}, u32[]{:S(2)}) %collective-permute-start) | collective-permute-done | bytes 32800 | tf_op jit(solution)/shard_map/ppermute | solution.py:132
  22.9 0.0 collective-permute-done.1.inverse_ref
  22.9 0.0 all-to-all-done.arrived_ref
  22.9 1.7 %last_section.1 = (f32[2,16,512]{2,1,0:T(8,128)S(1)}, f32[16,16,128]{2,1,0:T(8,128)}) custom-call(f32[16,24,128]{2,1,0:T(8,128)S(1)} %all-to-all-done.arrived_ref, f32[16,512]{1,0:T(8,128)S(1)} %collective-permute-done.rhs_ref, f32[4,128,128]{2,1,0:T(8,128)S(1)} %collective-permute-done.1.inverse_ref), custom_call_target="tpu_custom_call" | custom-call | tf_op jit(solution)/shard_map/last_section/pallas_call | solution.py:145
  24.6 5.7 %all-to-all-start.1 = ((f32[16,16,128]{2,1,0:T(8,128)}), f32[16,16,128]{2,1,0:T(8,128)S(1)}, u32[]{:S(2)}, u32[]{:S(2)}) async-start(f32[16,16,128]{2,1,0:T(8,128)} %get-tuple-element.9), calls=%async_computation.1 | async-start | bytes 262144 | tf_op jit(solution)/shard_map/all_to_all | solution.py:129
  30.4 1.6 %collective-permute-start.2 = (f32[2,16,512]{2,1,0:T(8,128)S(1)}, f32[2,16,512]{2,1,0:T(8,128)S(1)}, u32[]{:S(2)}, u32[]{:S(2)}) collective-permute-start(f32[2,16,512]{2,1,0:T(8,128)S(1)} %get-tuple-element.7), channel_id=1, source_target_pairs={{0,16},{16,0},{1,17},{17,1},{2,18},{18,2},{3,19},{19,3},{4,20},{20... | collective-permute-start | bytes 196616 | tf_op jit(solution)/shard_map/ppermute | solution.py:158
  31.9 6.4 %all-to-all-done.1.picked_ref = f32[16,16,128]{2,1,0:T(8,128)S(1)} async-done(((f32[16,16,128]{2,1,0:T(8,128)}), f32[16,16,128]{2,1,0:T(8,128)S(1)}, u32[]{:S(2)}, u32[]{:S(2)}) %all-to-all-start.1) | async-done | bytes 131104 | tf_op jit(solution)/shard_map/all_to_all | solution.py:129
  38.3 0.0 copy-done.1
  38.3 2.6 %backward.1 = f32[16,512]{1,0:T(8,128)S(1)} custom-call(s32[4,2]{1,0:T(4,128)S(1)} %copy.6.targets_ref, f32[16,16,128]{2,1,0:T(8,128)S(1)} %all-to-all-done.1.picked_ref, f32[16,512]{1,0:T(8,128)S(1)} %get-tuple-element.8.values_ref, f32[4,128,128]{2,1,0:T(8,128)S(1)} %copy-done.3, f32[4,2,128,128]{3,2,1,0:T(8,128)S(1)} %copy-done.1), custom_call_target="tpu_custom_call" | custom-call | tf_op jit(solution)/shard_map/backward/pallas_call | solution.py:150
  40.9 0.0 collective-permute-done.2
  40.9 0.7 %fusion = (f32[16,512]{1,0:T(8,128)}, f32[16,512]{1,0:T(8,128)}) fusion(f32[16,512]{1,0:T(8,128)S(1)} %backward.1, f32[2,16,512]{2,1,0:T(8,128)S(1)} %collective-permute-done.2, pred[]{:T(512)S(6)} %eq.3, f32[16,512]{1,0:T(8,128)S(1)} %get-tuple-element.8.values_ref), kind=kLoop, calls=%fused_computation.1 | loop fusion | flops 16384 | bytes 196609 | tf_op jit(solution)/shard_map/jit(_where)/select_n | solution.py:160
  (1 shorter events, 0.0 us)
Async XLA Ops:
  0.6 0.8 %copy-start.4 = (f32[16,512]{1,0:T(8,128)S(1)}, f32[16,512]{1,0:T(8,128)}, u32[]{:S(2)}) copy-start(f32[16,512]{1,0:T(8,128)} %rhs_ref.1) | copy-start | bytes 98308
  1.4 1.0 %copy-start = (f32[4,2,128,128]{3,2,1,0:T(8,128)S(1)}, f32[4,2,128,128]{3,2,1,0:T(8,128)}, u32[]{:S(2)}) copy-start(f32[4,2,128,128]{3,2,1,0:T(8,128)} %couplings_ref.3) | copy-start | bytes 1572868
  2.5 0.9 %copy-start.2 = (f32[4,128,128]{2,1,0:T(8,128)S(1)}, f32[4,128,128]{2,1,0:T(8,128)}, u32[]{:S(2)}) copy-start(f32[4,128,128]{2,1,0:T(8,128)} %inverse_ref.3) | copy-start | bytes 786436
  6.0 7.5 %copy-start.3 = (f32[4,128,128]{2,1,0:T(8,128)S(1)}, f32[4,128,128]{2,1,0:T(8,128)}, u32[]{:S(2)}) copy-start(f32[4,128,128]{2,1,0:T(8,128)} %inverse_ref.3) | copy-start | bytes 786436
  6.0 32.3 %copy-start.1 = (f32[4,2,128,128]{3,2,1,0:T(8,128)S(1)}, f32[4,2,128,128]{3,2,1,0:T(8,128)}, u32[]{:S(2)}) copy-start(f32[4,2,128,128]{3,2,1,0:T(8,128)} %couplings_ref.3) | copy-start | bytes 1572868
  6.0 16.9 %all-to-all-start = ((f32[16,24,128]{2,1,0:T(8,128)}), f32[16,24,128]{2,1,0:T(8,128)S(1)}, u32[]{:S(2)}, u32[]{:S(2)}) async-start(f32[16,24,128]{2,1,0:T(8,128)} %get-tuple-element.6), calls=%async_computation | async-start | bytes 393216 | tf_op jit(solution)/shard_map/all_to_all | solution.py:129
  13.5 9.4 %collective-permute-start.1 = (f32[4,128,128]{2,1,0:T(8,128)S(1)}, f32[4,128,128]{2,1,0:T(8,128)S(1)}, u32[]{:S(2)}, u32[]{:S(2)}) collective-permute-start(f32[4,128,128]{2,1,0:T(8,128)S(1)} %copy-done.3), channel_id=1, source_target_pairs={{0,16},{16,0},{1,17},{17,1},{2,18},{18,2},{3,19},{19,3},{4,20},{20... | collective-permute-start | bytes 786440 | tf_op jit(solution)/shard_map/ppermute | solution.py:131
  15.1 7.9 %collective-permute-start = (f32[16,512]{1,0:T(8,128)S(1)}, f32[16,512]{1,0:T(8,128)S(1)}, u32[]{:S(2)}, u32[]{:S(2)}) collective-permute-start(f32[16,512]{1,0:T(8,128)S(1)} %copy-done.4), channel_id=1, source_target_pairs={{0,16},{16,0},{1,17},{17,1},{2,18},{18,2},{3,19},{19,3},{4,20},{20... | collective-permute-start | bytes 98312 | tf_op jit(solution)/shard_map/ppermute | solution.py:132
  24.6 13.7 %all-to-all-start.1 = ((f32[16,16,128]{2,1,0:T(8,128)}), f32[16,16,128]{2,1,0:T(8,128)S(1)}, u32[]{:S(2)}, u32[]{:S(2)}) async-start(f32[16,16,128]{2,1,0:T(8,128)} %get-tuple-element.9), calls=%async_computation.1 | async-start | bytes 262144 | tf_op jit(solution)/shard_map/all_to_all | solution.py:129
  30.4 10.6 %collective-permute-start.2 = (f32[2,16,512]{2,1,0:T(8,128)S(1)}, f32[2,16,512]{2,1,0:T(8,128)S(1)}, u32[]{:S(2)}, u32[]{:S(2)}) collective-permute-start(f32[2,16,512]{2,1,0:T(8,128)S(1)} %get-tuple-element.7), channel_id=1, source_target_pairs={{0,16},{16,0},{1,17},{17,1},{2,18},{18,2},{3,19},{19,3},{4,20},{20... | collective-permute-start | bytes 196616 | tf_op jit(solution)/shard_map/ppermute | solution.py:158

commit v2 on v1

v2 whole, which is shorter than its diff:
```python
import jax
import jax.numpy as jnp
from jax import lax
from jax.experimental import pallas as pl
from jax.experimental.pallas import tpu as pltpu
from jax.sharding import PartitionSpec as P

VMEM = pl.BlockSpec(memory_space=pltpu.VMEM)
COVER = 20_000_000_000
HBM = pl.BlockSpec(memory_space=pltpu.HBM)


def split(value):
    high = value.astype(jnp.bfloat16)
    return high, (value - high.astype(jnp.float32)).astype(jnp.bfloat16)


def times(left, right, contracted=0):
    rows = left.shape[0]
    left_high, left_low = split(left)
    right_high, right_low = right

    def dot(a, b):
        numbers = (((1,), (contracted,)), ((), ()))
        return lax.dot_general(a, b, numbers, preferred_element_type=jnp.float32)

    both = dot(jnp.concatenate([left_high, left_low], axis=0), right_high)
    return both[:rows] + (both[rows:] + dot(left_high, right_low))


def times_transposed(left, right):
    return times(left, right, 1)


def kernel_call(kernel, out_shape, specs, name, flops=None, scratch=(), vmem=16 * 2**20):
    cost = None
    if flops is not None:
        cost = pl.CostEstimate(flops=flops, bytes_accessed=0, transcendentals=0)
    return pl.pallas_call(
        kernel,
        out_shape=out_shape,
        in_specs=specs,
        out_specs=jax.tree.map(lambda _: VMEM, out_shape),
        compiler_params=pltpu.CompilerParams(vmem_limit_bytes=vmem),
        cost_estimate=cost,
        scratch_shapes=scratch,
        name=name,
    )


def split_kernel(*refs):
    count = len(refs) // 3
    for i in range(count):
        refs[count + 2 * i][...], refs[count + 2 * i + 1][...] = split(refs[i][...])


def split_arrays(arrays, flops):
    out = tuple(jax.ShapeDtypeStruct(a.shape, jnp.bfloat16) for a in arrays for _ in range(2))
    return kernel_call(split_kernel, out, [VMEM] * len(arrays), "split_weights", flops)(*arrays)


def lane_blocks(width, count):
    return [slice(i * width, (i + 1) * width) for i in range(count)]


def summed_by_row(arrived_ref, local_count, rhs_count):
    stride = rhs_count + 1
    sums = [None] * local_count
    for start in range(0, arrived_ref.shape[0], stride):
        block = arrived_ref[start : start + rhs_count, :]
        row = arrived_ref[start + rhs_count : start + stride, :]
        for local in range(local_count):
            term = jnp.where(row == local, block, 0.0)
            sums[local] = term if sums[local] is None else sums[local] + term
    return sums


def place_answers(arrived_ref, answers_ref, solved, rhs_count):
    stride = rhs_count + 1
    for column in range(answers_ref.shape[0]):
        last = (column + 1) * stride
        row = arrived_ref[last - 1 : last, :]
        answer = jnp.zeros_like(solved[0])
        for local, values in enumerate(solved):
            answer = jnp.where(row == local, values, answer)
        answers_ref[column] = answer


def forward_kernel(targets_hbm, rhs_hbm, inverse_hbm, couplings_hbm, *rest):
    *incoming_ref, values_ref, passed_ref, owners_ref, out_ref = rest[:-5]
    targets_ref, rhs_ref, inverse_ref, couplings_ref, sems = rest[-5:]
    sources = (targets_hbm, rhs_hbm, inverse_hbm, couplings_hbm)
    places = (targets_ref, rhs_ref, inverse_ref, couplings_ref)
    copies = [
        pltpu.make_async_copy(source, place, sems.at[i])
        for i, (source, place) in enumerate(zip(sources, places))
    ]
    for copy in copies:
        copy.start()
    out_ref[...] = jnp.full(out_ref.shape, -1.0, jnp.float32)
    local_count, width, _ = inverse_ref.shape
    fanout = couplings_ref.shape[1]
    rhs_count = rhs_ref.shape[0]
    stride = rhs_count + 1
    copies[1].wait()
    copies[2].wait()
    passed_ref[...] = rhs_ref[...]
    solved = []
    for local, lanes in enumerate(lane_blocks(width, local_count)):
        source = rhs_ref[:, lanes]
        if incoming_ref:
            source = source - incoming_ref[0][:, lanes]
        solved.append(times(source, split(inverse_ref[local])))
        values_ref[:, lanes] = solved[local]
    copies[0].wait()
    copies[3].wait()
    for local in range(local_count):
        for k in range(fanout):
            target = targets_ref[k, local]
            owner = target // local_count
            start = owner * stride
            row = jnp.full((1, width), target % local_count, jnp.int32)
            out_ref[pl.ds(start, rhs_count), :] = times(solved[local], split(couplings_ref[local, k]))
            out_ref[pl.ds(start + rhs_count, 1), :] = row.astype(jnp.float32)
            pair = local * fanout + k
            owners_ref[pair : pair + 1, :] = jnp.full((1, width), owner, jnp.int32)


def sum_kernel(arrived_ref, sums_ref):
    rhs_count, width = sums_ref.shape[0], arrived_ref.shape[1]
    lanes = lane_blocks(width, sums_ref.shape[1] // width)
    for local, total in enumerate(summed_by_row(arrived_ref, len(lanes), rhs_count)):
        sums_ref[:, lanes[local]] = total


def last_kernel(arrived_ref, rhs_ref, high_ref, low_ref, pair_ref, answers_ref):
    local_count, width, _ = high_ref.shape
    rhs_count = rhs_ref.shape[0]
    sums = summed_by_row(arrived_ref, local_count, rhs_count)
    lanes = lane_blocks(width, local_count)
    inverse = [(high_ref[i], low_ref[i]) for i in range(local_count)]
    forward = [times(rhs_ref[:, lanes[i]] - sums[i], inverse[i]) for i in range(local_count)]
    backward = [times_transposed(forward[i], inverse[i]) for i in range(local_count)]
    for local in range(local_count):
        pair_ref[0, :, lanes[local]] = forward[local]
        pair_ref[1, :, lanes[local]] = backward[local]
    place_answers(arrived_ref, answers_ref, backward, rhs_count)


def place_kernel(arrived_ref, solved_ref, answers_ref):
    rhs_count, width = solved_ref.shape[0], arrived_ref.shape[1]
    lanes = lane_blocks(width, solved_ref.shape[1] // width)
    place_answers(arrived_ref, answers_ref, [solved_ref[:, lane] for lane in lanes], rhs_count)


def backward_kernel(
    owners_ref,
    picked_ref,
    values_ref,
    inverse_high_ref,
    inverse_low_ref,
    couplings_high_ref,
    couplings_low_ref,
    *rest,
):
    *pair_ref, solution_ref = rest
    if pair_ref:
        pair_ref, forward_ref = pair_ref
    local_count, width, _ = inverse_high_ref.shape
    fanout = couplings_high_ref.shape[1]
    lanes = lane_blocks(width, local_count)

    def solve():
        blocks = [jnp.zeros(picked_ref.shape[1:], jnp.float32)] * (local_count * fanout)
        for column in range(picked_ref.shape[0]):
            block = picked_ref[column]
            for pair in range(local_count * fanout):
                chosen = owners_ref[pair : pair + 1, :] == column
                blocks[pair] = jnp.where(chosen, block, blocks[pair])
        sources = []
        for local in range(local_count):
            source = values_ref[:, lanes[local]]
            for k in range(fanout):
                coupling = (couplings_high_ref[local, k], couplings_low_ref[local, k])
                source = source - times_transposed(blocks[local * fanout + k], coupling)
            sources.append(source)
        for local in range(local_count):
            inverse = (inverse_high_ref[local], inverse_low_ref[local])
            solution_ref[:, lanes[local]] = times_transposed(sources[local], inverse)

    if not isinstance(pair_ref, list):
        is_last = lax.axis_index("section") == lax.axis_size("section") - 1

        @pl.when(is_last)
        def _():
            forward_ref[...] = pair_ref[0]
            solution_ref[...] = pair_ref[1]

        @pl.when(jnp.logical_not(is_last))
        def _():
            forward_ref[...] = values_ref[...]
            solve()

    else:
        solve()


def body(rhs, inverse_blocks, couplings, targets):
    sections = lax.axis_size("section")
    columns = lax.axis_size("col")
    my_section = lax.axis_index("section")
    local_count, width, _ = inverse_blocks.shape
    rhs_count = rhs.shape[0]
    stride = rhs_count + 1
    up = [(s, (s + 1) % sections) for s in range(sections)]
    down = [(s, (s - 1) % sections) for s in range(sections)]
    flat = jax.ShapeDtypeStruct(rhs.shape, jnp.float32)
    slots = jax.ShapeDtypeStruct((columns * stride, width), jnp.float32)
    answered = jax.ShapeDtypeStruct((columns, rhs_count, width), jnp.float32)
    pair = jax.ShapeDtypeStruct((2,) + rhs.shape, jnp.float32)
    owners = jax.ShapeDtypeStruct((local_count * couplings.shape[1], width), jnp.int32)
    aimed = targets.T
    inputs = (aimed, rhs, inverse_blocks, couplings)
    held = [pltpu.SMEM(aimed.shape, jnp.int32)]
    held += [pltpu.VMEM(a.shape, a.dtype) for a in inputs[1:]]
    held += [pltpu.SemaphoreType.DMA((len(inputs),))]

    def exchanged(value):
        return lax.all_to_all(value, "col", split_axis=0, concat_axis=0, tiled=True)

    next_inverse = lax.ppermute(inverse_blocks, "section", down)

    incoming = ()
    for step in range(sections - 1):
        values, passed, owner_rows, outgoing = kernel_call(
            forward_kernel,
            (flat, flat, owners, slots),
            [HBM] * len(inputs) + [VMEM] * len(incoming),
            "forward",
            scratch=held,
            vmem=60*2**20,
        )(*inputs, *incoming)
        arrived = exchanged(outgoing.reshape(columns, stride, 1, width)).reshape(slots.shape)
        if step < sections - 2:
            sums = kernel_call(sum_kernel, flat, [VMEM], "sum_rows")(arrived)
            moved = lax.ppermute(sums, "section", up)
            incoming = (jnp.where(my_section == 0, 0.0, moved),)

    next_rhs = lax.ppermute(passed, "section", down)
    next_split = split_arrays((next_inverse,), COVER)
    weights = split_arrays((inverse_blocks, couplings), COVER)
    last, answers = kernel_call(last_kernel, (pair, answered), [VMEM] * 4, "last_section")(
        arrived, next_rhs, *next_split
    )
    for step in range(sections - 1):
        picked = exchanged(answers)
        operands = (owner_rows, picked, values, *weights)
        if step < sections - 2:
            solved = kernel_call(backward_kernel, flat, [VMEM] * len(operands), "backward")(
                *operands
            )
            moved = lax.ppermute(solved, "section", down)
            following = jnp.where(my_section == sections - 2, last[1], moved)
            answers = kernel_call(place_kernel, answered, [VMEM, VMEM], "place")(arrived, following)

    final = lax.ppermute(last, "section", up)
    return kernel_call(backward_kernel, (flat, flat), [VMEM] * (len(operands) + 1), "backward_last")(
        *operands, final
    )


def solution(mesh):
    return jax.shard_map(
        body,
        mesh=mesh,
        in_specs=(
            P(None, ("section", "col")),
            P(("section", "col"), None, None),
            P(("section", "col"), None, None, None),
            P(("section", "col"), None),
        ),
        out_specs=(P(None, ("section", "col")), P(None, ("section", "col"))),
        check_vma=False,
    )
```

time: 42 us -> 34.5 us (0.82)
  starting transfers between devices: 16.9 us -> 13.7 us
  Pallas kernels: 6.87 us -> 4.5 us
  local copies, waits for them, and re-layouts: 2.77 us -> 0.69 us
  waiting for transfers between devices: 13.7 us -> 14.6 us
  other arithmetic: 0.67 us -> 0 us
    ppermute x1, waiting for transfers between devices: 7.32 us -> 3.32 us  [body(): next_rhs = lax.ppermute(passed, 'section', down)]
    all_to_all x2, starting transfers between devices: 13.2 us -> 9.46 us  [exchanged(): return lax.all_to_all(value, 'col', split_axis=0, concat_axis=0, tiled=True)]
    ppermute x1, waiting for transfers between devices: 0.01 us -> 3.59 us  [body(): final = lax.ppermute(last, 'section', up)]
    pallas_call x3 -> x5, Pallas kernels: 6.87 us -> 4.5 us  [the longest x1 2.14 us: body(): kernel_call(forward_kernel, (flat, flat, owners, slots), [HBM] * len(inpu...]
    unnamed x11 -> x10, local copies, waits for them, and re-layouts: 2.77 us -> 0.69 us
    ppermute x1, starting transfers between devices: 1.56 us -> 3 us  [body(): next_inverse = lax.ppermute(inverse_blocks, 'section', down)]
    all_to_all x2, waiting for transfers between devices: 6.38 us -> 7.64 us  [exchanged(): return lax.all_to_all(value, 'col', split_axis=0, concat_axis=0, tiled=True)]
    ppermute x1, starting transfers between devices: 1.56 us -> 0.6 us  [body(): final = lax.ppermute(last, 'section', up)]
  transfers between devices with their start and end apart: 5 -> 5, of which waited for: 2 -> 4; matrix products, arithmetic and copies ran while one was open for 0% -> 0% of each run, Pallas kernels for 6% -> 7%
where the time goes in v2:
time: 34.5 us; the launch traced here: 34.1 us
  waiting for transfers between devices  14.6 us (42%)
  starting transfers between devices  13.7 us (40%)
  Pallas kernels  4.5 us (13%)
  local copies, waits for them, and re-layouts  0.69 us (2%)
  between operations  0.69 us (2%)
    all_to_all x2, starting transfers between devices, exchanged(): return lax.all_to_all(value, 'col', split_axis=0, concat_axis=0, tiled=True)  9.46 us
    all_to_all x2, waiting for transfers between devices, exchanged(): return lax.all_to_all(value, 'col', split_axis=0, concat_axis=0, tiled=True)  7.64 us
    ppermute x1, waiting for transfers between devices, body(): final = lax.ppermute(last, 'section', up)  3.59 us
    ppermute x1, waiting for transfers between devices, body(): next_rhs = lax.ppermute(passed, 'section', down)  3.32 us
    ppermute x1, starting transfers between devices, body(): next_inverse = lax.ppermute(inverse_blocks, 'section', down)  3 us
    pallas_call x1, Pallas kernels, body(): kernel_call(forward_kernel, (flat, flat, owners, slots), [HBM] * len(inpu...  2.14 us
    pallas_call x1, Pallas kernels, body(): kernel_call(backward_kernel, (flat, flat), [VMEM] * (len(operands) + 1),...  1.15 us
    pallas_call x1, Pallas kernels, body(): kernel_call(last_kernel, (pair, answered), [VMEM] * 4, 'last_section')  1.05 us
  transfers between devices with their start and end apart: 5, of which 4 were waited for; matrix products, arithmetic and copies ran while one was open for 0% of the time, Pallas kernels for 7%

profile of v2, /device:TPU:0, one launch (start us, length us, event | category | flops | bytes accessed | tf_op | source)
XLA Modules:
  0.0 34.1 jit_solution(2888514871182151611)
XLA Ops:
  0.6 3.0 %collective-permute-start.1 = (f32[4,128,128]{2,1,0:T(8,128)}, f32[4,128,128]{2,1,0:T(8,128)S(1)}, u32[]{:S(2)}, u32[]{:S(2)}) collective-permute-start(f32[4,128,128]{2,1,0:T(8,128)} %refs_0_.1), channel_id=1, source_target_pairs={{0,16},{16,0},{1,17},{17,1},{2,18},{18,2},{3,19},{19,3},{4,20},{20... | collective-permute-start | bytes 786440 | tf_op jit(solution)/shard_map/ppermute | solution.py:231
  3.6 2.1 %forward.1 = (f32[16,512]{1,0:T(8,128)}, f32[16,512]{1,0:T(8,128)}, s32[8,128]{1,0:T(8,128)}, f32[272,128]{1,0:T(8,128)}) custom-call(s32[2,4]{1,0:T(2,128)} %bitcast.5, f32[16,512]{1,0:T(8,128)} %rhs_hbm.1, f32[4,128,128]{2,1,0:T(8,128)} %refs_0_.1, f32[4,2,128,128]{3,2,1,0:T(8,128)} %refs_1_.1), custom_call_target="tpu_custom_call" | custom-call | tf_op jit(solution)/shard_map/forward/pallas_call | solution.py:235
  5.8 0.0 copy-start.4
  5.8 6.0 %all-to-all-start = ((f32[16,17,1,128]{3,2,1,0:T(1,128)}), f32[16,17,1,128]{3,2,1,0:T(1,128)S(1)}, u32[]{:S(2)}, u32[]{:S(2)}) async-start(f32[16,17,1,128]{3,2,1,0:T(1,128)} %bitcast.4), calls=%async_computation | async-start | bytes 278528 | tf_op jit(solution)/shard_map/all_to_all | solution.py:229
  11.7 0.0 copy-done.4
  11.8 0.6 %collective-permute-start = (f32[16,512]{1,0:T(8,128)S(1)}, f32[16,512]{1,0:T(8,128)S(1)}, u32[]{:S(2)}, u32[]{:S(2)}) collective-permute-start(f32[16,512]{1,0:T(8,128)S(1)} %copy-done.4), channel_id=1, source_target_pairs={{0,16},{16,0},{1,17},{17,1},{2,18},{18,2},{3,19},{19,3},{4,20},{20... | collective-permute-start | bytes 98312 | tf_op jit(solution)/shard_map/ppermute | solution.py:249
  12.4 0.0 collective-permute-done.1.refs_0_
  12.4 0.0 copy-start.1
  12.4 0.0 copy-start
  12.4 3.3 %collective-permute-done.rhs_ref = f32[16,512]{1,0:T(8,128)S(1)} collective-permute-done((f32[16,512]{1,0:T(8,128)S(1)}, f32[16,512]{1,0:T(8,128)S(1)}, u32[]{:S(2)}, u32[]{:S(2)}) %collective-permute-start) | collective-permute-done | bytes 32800 | tf_op jit(solution)/shard_map/ppermute | solution.py:249
  15.7 4.1 %all-to-all-done = f32[16,17,1,128]{3,2,1,0:T(1,128)S(1)} async-done(((f32[16,17,1,128]{3,2,1,0:T(1,128)}), f32[16,17,1,128]{3,2,1,0:T(1,128)S(1)}, u32[]{:S(2)}, u32[]{:S(2)}) %all-to-all-start) | async-done | bytes 139296 | tf_op jit(solution)/shard_map/all_to_all | solution.py:229
  19.8 1.1 %last_section.1 = (f32[2,16,512]{2,1,0:T(8,128)S(1)}, f32[16,16,128]{2,1,0:T(8,128)}) custom-call(f32[272,128]{1,0:T(8,128)S(1)} %bitcast.3, f32[16,512]{1,0:T(8,128)S(1)} %collective-permute-done.rhs_ref, bf16[4,128,128]{2,1,0:T(8,128)(2,1)S(1)} %get-tuple-element.17.high_ref, bf16[4,128,128]{2,1,0:T(8,128)(2,1)S(1)} %get-tuple-element.18.low_ref), custom_call_target="tpu_custom_call" | custom-call | tf_op jit(solution)/shard_map/last_section/pallas_call | solution.py:252
  20.9 3.5 %all-to-all-start.1 = ((f32[16,16,128]{2,1,0:T(8,128)}), f32[16,16,128]{2,1,0:T(8,128)S(1)}, u32[]{:S(2)}, u32[]{:S(2)}) async-start(f32[16,16,128]{2,1,0:T(8,128)} %get-tuple-element.19), calls=%async_computation.1 | async-start | bytes 262144 | tf_op jit(solution)/shard_map/all_to_all | solution.py:229
  24.4 0.6 %collective-permute-start.2 = (f32[2,16,512]{2,1,0:T(8,128)S(1)}, f32[2,16,512]{2,1,0:T(8,128)S(1)}, u32[]{:S(2)}, u32[]{:S(2)}) collective-permute-start(f32[2,16,512]{2,1,0:T(8,128)S(1)} %get-tuple-element.25), channel_id=1, source_target_pairs={{0,16},{16,0},{1,17},{17,1},{2,18},{18,2},{3,19},{19,3},{4,20},{20... | collective-permute-start | bytes 196616 | tf_op jit(solution)/shard_map/ppermute | solution.py:266
  25.0 0.0 copy-done.1
  25.0 0.0 copy-done
  25.0 0.0 copy-start.2
  25.0 0.1 split_weights.3
  25.1 3.6 %collective-permute-done.2.rest_0_ = f32[2,16,512]{2,1,0:T(8,128)S(1)} collective-permute-done((f32[2,16,512]{2,1,0:T(8,128)S(1)}, f32[2,16,512]{2,1,0:T(8,128)S(1)}, u32[]{:S(2)}, u32[]{:S(2)}) %collective-permute-start.2) | collective-permute-done | bytes 65568 | tf_op jit(solution)/shard_map/ppermute | solution.py:266
  28.7 3.6 %all-to-all-done.1.picked_ref = f32[16,16,128]{2,1,0:T(8,128)S(1)} async-done(((f32[16,16,128]{2,1,0:T(8,128)}), f32[16,16,128]{2,1,0:T(8,128)S(1)}, u32[]{:S(2)}, u32[]{:S(2)}) %all-to-all-start.1) | async-done | bytes 131104 | tf_op jit(solution)/shard_map/all_to_all | solution.py:229
  32.3 0.0 copy-start.3
  32.3 0.0 copy-done.2
  32.3 0.7 %copy-done.3 = s32[8,128]{1,0:T(8,128)S(1)} copy-done((s32[8,128]{1,0:T(8,128)S(1)}, s32[8,128]{1,0:T(8,128)}, u32[]{:S(2)}) %copy-start.3) | copy-done | bytes 4120
  33.0 1.2 %backward_last.1 = (f32[16,512]{1,0:T(8,128)}, f32[16,512]{1,0:T(8,128)}) custom-call(s32[8,128]{1,0:T(8,128)S(1)} %copy-done.3, f32[16,16,128]{2,1,0:T(8,128)S(1)} %all-to-all-done.1.picked_ref, f32[16,512]{1,0:T(8,128)S(1)} %copy-done.2, bf16[4,128,128]{2,1,0:T(8,128)(2,1)S(1)} %get-tuple-element.21.inverse_high_ref, ...), custom_call_target="tpu_custom_call" | custom-call | tf_op jit(solution)/shard_map/backward_last/pallas_call | solution.py:267
  (1 shorter events, 0.0 us)
Async XLA Ops:
  0.6 11.7 %collective-permute-start.1 = (f32[4,128,128]{2,1,0:T(8,128)}, f32[4,128,128]{2,1,0:T(8,128)S(1)}, u32[]{:S(2)}, u32[]{:S(2)}) collective-permute-start(f32[4,128,128]{2,1,0:T(8,128)} %refs_0_.1), channel_id=1, source_target_pairs={{0,16},{16,0},{1,17},{17,1},{2,18},{18,2},{3,19},{19,3},{4,20},{20... | collective-permute-start | bytes 786440 | tf_op jit(solution)/shard_map/ppermute | solution.py:231
  5.8 6.0 %copy-start.4 = (f32[16,512]{1,0:T(8,128)S(1)}, f32[16,512]{1,0:T(8,128)}, u32[]{:S(2)}) copy-start(f32[16,512]{1,0:T(8,128)} %get-tuple-element.16) | copy-start | bytes 98308
  5.8 14.0 %all-to-all-start = ((f32[16,17,1,128]{3,2,1,0:T(1,128)}), f32[16,17,1,128]{3,2,1,0:T(1,128)S(1)}, u32[]{:S(2)}, u32[]{:S(2)}) async-start(f32[16,17,1,128]{3,2,1,0:T(1,128)} %bitcast.4), calls=%async_computation | async-start | bytes 278528 | tf_op jit(solution)/shard_map/all_to_all | solution.py:229
  11.8 4.0 %collective-permute-start = (f32[16,512]{1,0:T(8,128)S(1)}, f32[16,512]{1,0:T(8,128)S(1)}, u32[]{:S(2)}, u32[]{:S(2)}) collective-permute-start(f32[16,512]{1,0:T(8,128)S(1)} %copy-done.4), channel_id=1, source_target_pairs={{0,16},{16,0},{1,17},{17,1},{2,18},{18,2},{3,19},{19,3},{4,20},{20... | collective-permute-start | bytes 98312 | tf_op jit(solution)/shard_map/ppermute | solution.py:249
  12.4 12.6 %copy-start.1 = (f32[4,128,128]{2,1,0:T(8,128)S(1)}, f32[4,128,128]{2,1,0:T(8,128)}, u32[]{:S(2)}) copy-start(f32[4,128,128]{2,1,0:T(8,128)} %refs_0_.1) | copy-start | bytes 786436
  12.4 12.6 %copy-start = (f32[4,2,128,128]{3,2,1,0:T(8,128)S(1)}, f32[4,2,128,128]{3,2,1,0:T(8,128)}, u32[]{:S(2)}) copy-start(f32[4,2,128,128]{3,2,1,0:T(8,128)} %refs_1_.1) | copy-start | bytes 1572868
  20.9 11.4 %all-to-all-start.1 = ((f32[16,16,128]{2,1,0:T(8,128)}), f32[16,16,128]{2,1,0:T(8,128)S(1)}, u32[]{:S(2)}, u32[]{:S(2)}) async-start(f32[16,16,128]{2,1,0:T(8,128)} %get-tuple-element.19), calls=%async_computation.1 | async-start | bytes 262144 | tf_op jit(solution)/shard_map/all_to_all | solution.py:229
  24.4 4.3 %collective-permute-start.2 = (f32[2,16,512]{2,1,0:T(8,128)S(1)}, f32[2,16,512]{2,1,0:T(8,128)S(1)}, u32[]{:S(2)}, u32[]{:S(2)}) collective-permute-start(f32[2,16,512]{2,1,0:T(8,128)S(1)} %get-tuple-element.25), channel_id=1, source_target_pairs={{0,16},{16,0},{1,17},{17,1},{2,18},{18,2},{3,19},{19,3},{4,20},{20... | collective-permute-start | bytes 196616 | tf_op jit(solution)/shard_map/ppermute | solution.py:266
  25.0 7.3 %copy-start.2 = (f32[16,512]{1,0:T(8,128)S(1)}, f32[16,512]{1,0:T(8,128)}, u32[]{:S(2)}) copy-start(f32[16,512]{1,0:T(8,128)} %get-tuple-element.20.values_ref) | copy-start | bytes 98308
  32.3 0.7 %copy-start.3 = (s32[8,128]{1,0:T(8,128)S(1)}, s32[8,128]{1,0:T(8,128)}, u32[]{:S(2)}) copy-start(s32[8,128]{1,0:T(8,128)} %get-tuple-element.14.owners_ref) | copy-start | bytes 12292

commit v3 on v2

--- a/solution.py
+++ b/solution.py
@@ -1,3 +1,5 @@
+import functools
+
 import jax
 import jax.numpy as jnp
 from jax import lax
@@ -48,15 +50,21 @@
     )
 
 
-def split_kernel(*refs):
-    count = len(refs) // 3
-    for i in range(count):
-        refs[count + 2 * i][...], refs[count + 2 * i + 1][...] = split(refs[i][...])
-
-
-def split_arrays(arrays, flops):
-    out = tuple(jax.ShapeDtypeStruct(a.shape, jnp.bfloat16) for a in arrays for _ in range(2))
-    return kernel_call(split_kernel, out, [VMEM] * len(arrays), "split_weights", flops)(*arrays)
+def split_kernel(count, kept, *refs):
+    passed, arrays, refs = refs[:kept], refs[kept : kept + count], refs[kept + count :]
+    for i in range(kept):
+        refs[i][...] = passed[i][...]
+    for i, array in enumerate(arrays):
+        at = kept + 2 * i
+        refs[at][...], refs[at + 1][...] = split(array[...])
+
+
+def split_arrays(arrays, flops, kept=()):
+    out = tuple(jax.ShapeDtypeStruct(a.shape, a.dtype) for a in kept)
+    out += tuple(jax.ShapeDtypeStruct(a.shape, jnp.bfloat16) for a in arrays for _ in range(2))
+    kernel = functools.partial(split_kernel, len(arrays), len(kept))
+    specs = [VMEM] * (len(kept) + len(arrays))
+    return kernel_call(kernel, out, specs, "split_weights", flops)(*kept, *arrays)
 
 
 def lane_blocks(width, count):
@@ -87,7 +95,7 @@
 
 
 def forward_kernel(targets_hbm, rhs_hbm, inverse_hbm, couplings_hbm, *rest):
-    *incoming_ref, values_ref, passed_ref, owners_ref, out_ref = rest[:-5]
+    *incoming_ref, values_ref, passed_ref, slots_ref, out_ref = rest[:-5]
     targets_ref, rhs_ref, inverse_ref, couplings_ref, sems = rest[-5:]
     sources = (targets_hbm, rhs_hbm, inverse_hbm, couplings_hbm)
     places = (targets_ref, rhs_ref, inverse_ref, couplings_ref)
@@ -102,6 +110,7 @@
     fanout = couplings_ref.shape[1]
     rhs_count = rhs_ref.shape[0]
     stride = rhs_count + 1
+    columns = out_ref.shape[0] // stride
     copies[1].wait()
     copies[2].wait()
     passed_ref[...] = rhs_ref[...]
@@ -117,13 +126,13 @@
     for local in range(local_count):
         for k in range(fanout):
             target = targets_ref[k, local]
-            owner = target // local_count
-            start = owner * stride
+            slot = columns - 1 - target // local_count
+            start = slot * stride
             row = jnp.full((1, width), target % local_count, jnp.int32)
             out_ref[pl.ds(start, rhs_count), :] = times(solved[local], split(couplings_ref[local, k]))
             out_ref[pl.ds(start + rhs_count, 1), :] = row.astype(jnp.float32)
             pair = local * fanout + k
-            owners_ref[pair : pair + 1, :] = jnp.full((1, width), owner, jnp.int32)
+            slots_ref[pair : pair + 1, :] = jnp.full((1, width), slot, jnp.int32)
 
 
 def sum_kernel(arrived_ref, sums_ref):
@@ -154,7 +163,7 @@
 
 
 def backward_kernel(
-    owners_ref,
+    slots_ref,
     picked_ref,
     values_ref,
     inverse_high_ref,
@@ -175,7 +184,7 @@
         for column in range(picked_ref.shape[0]):
             block = picked_ref[column]
             for pair in range(local_count * fanout):
-                chosen = owners_ref[pair : pair + 1, :] == column
+                chosen = slots_ref[pair : pair + 1, :] == column
                 blocks[pair] = jnp.where(chosen, block, blocks[pair])
         sources = []
         for local in range(local_count):
@@ -225,14 +234,18 @@
     held += [pltpu.VMEM(a.shape, a.dtype) for a in inputs[1:]]
     held += [pltpu.SemaphoreType.DMA((len(inputs),))]
 
+    members = [list(range(columns))[::-1]]
+
     def exchanged(value):
-        return lax.all_to_all(value, "col", split_axis=0, concat_axis=0, tiled=True)
+        return lax.all_to_all(
+            value, "col", split_axis=0, concat_axis=0, tiled=True, axis_index_groups=members
+        )
 
     next_inverse = lax.ppermute(inverse_blocks, "section", down)
 
     incoming = ()
     for step in range(sections - 1):
-        values, passed, owner_rows, outgoing = kernel_call(
+        values, passed, slot_rows, outgoing = kernel_call(
             forward_kernel,
             (flat, flat, owners, slots),
             [HBM] * len(inputs) + [VMEM] * len(incoming),
@@ -248,13 +261,15 @@
 
     next_rhs = lax.ppermute(passed, "section", down)
     next_split = split_arrays((next_inverse,), COVER)
-    weights = split_arrays((inverse_blocks, couplings), COVER)
+    slot_rows, values, *weights = split_arrays(
+        (inverse_blocks, couplings), COVER, (slot_rows, values)
+    )
     last, answers = kernel_call(last_kernel, (pair, answered), [VMEM] * 4, "last_section")(
         arrived, next_rhs, *next_split
     )
     for step in range(sections - 1):
         picked = exchanged(answers)
-        operands = (owner_rows, picked, values, *weights)
+        operands = (slot_rows, picked, values, *weights)
         if step < sections - 2:
             solved = kernel_call(backward_kernel, flat, [VMEM] * len(operands), "backward")(
                 *operands

time: 34.5 us -> 30.4 us (0.88)
  waiting for transfers between devices: 14.6 us -> 7.3 us
  starting transfers between devices: 13.7 us -> 17.5 us
  local copies, waits for them, and re-layouts: 0.69 us -> 0.08 us
    all_to_all x2, waiting for transfers between devices: 7.64 us -> 0.43 us  [exchanged(): lax.all_to_all(value, 'col', split_axis=0, concat_axis=0, tiled=True, axi...]
    all_to_all x2, starting transfers between devices: 9.46 us -> 13.3 us  [exchanged(): lax.all_to_all(value, 'col', split_axis=0, concat_axis=0, tiled=True, axi...]
    unnamed x10, local copies, waits for them, and re-layouts: 0.69 us -> 0.08 us
  transfers between devices with their start and end apart: 5 -> 5, of which waited for: 4 -> 3; matrix products, arithmetic and copies ran while one was open for 0% -> 0% of each run, Pallas kernels for 7% -> 8%
where the time goes in v3:
time: 30.4 us; the launch traced here: 30 us
  starting transfers between devices  17.5 us (58%)
  waiting for transfers between devices  7.3 us (24%)
  Pallas kernels  4.49 us (15%)
  between operations  0.68 us (2%)
    all_to_all x2, starting transfers between devices, exchanged(): lax.all_to_all(value, 'col', split_axis=0, concat_axis=0, tiled=True, axi...  13.3 us
    ppermute x1, waiting for transfers between devices, body(): final = lax.ppermute(last, 'section', up)  3.54 us
    ppermute x1, waiting for transfers between devices, body(): next_rhs = lax.ppermute(passed, 'section', down)  3.32 us
    ppermute x1, starting transfers between devices, body(): next_inverse = lax.ppermute(inverse_blocks, 'section', down)  3 us
    pallas_call x1, Pallas kernels, body(): kernel_call(forward_kernel, (flat, flat, owners, slots), [HBM] * len(inpu...  2.14 us
    pallas_call x1, Pallas kernels, body(): kernel_call(backward_kernel, (flat, flat), [VMEM] * (len(operands) + 1),...  1.15 us
    pallas_call x1, Pallas kernels, body(): kernel_call(last_kernel, (pair, answered), [VMEM] * 4, 'last_section')  1.04 us
  transfers between devices with their start and end apart: 5, of which 3 were waited for; matrix products, arithmetic and copies ran while one was open for 0% of the time, Pallas kernels for 8%

profile of v3, /device:TPU:0, one launch (start us, length us, event | category | flops | bytes accessed | tf_op | source)
XLA Modules:
  0.0 30.0 jit_solution(6342633002050144327)
XLA Ops:
  0.6 3.0 %collective-permute-start.1 = (f32[4,128,128]{2,1,0:T(8,128)}, f32[4,128,128]{2,1,0:T(8,128)S(1)}, u32[]{:S(2)}, u32[]{:S(2)}) collective-permute-start(f32[4,128,128]{2,1,0:T(8,128)} %refs_2_.1), channel_id=1, source_target_pairs={{0,16},{16,0},{1,17},{17,1},{2,18},{18,2},{3,19},{19,3},{4,20},{20... | collective-permute-start | bytes 786440 | tf_op jit(solution)/shard_map/ppermute | solution.py:244
  3.6 2.1 %forward.1 = (f32[16,512]{1,0:T(8,128)}, f32[16,512]{1,0:T(8,128)}, s32[8,128]{1,0:T(8,128)}, f32[272,128]{1,0:T(8,128)}) custom-call(s32[2,4]{1,0:T(2,128)} %bitcast.5, f32[16,512]{1,0:T(8,128)} %rhs_hbm.1, f32[4,128,128]{2,1,0:T(8,128)} %refs_2_.1, f32[4,2,128,128]{3,2,1,0:T(8,128)} %refs_3_.1), custom_call_target="tpu_custom_call" | custom-call | tf_op jit(solution)/shard_map/forward/pallas_call | solution.py:248
  5.8 0.0 copy-start.4
  5.8 7.2 %all-to-all-start = ((f32[16,17,1,128]{3,2,1,0:T(1,128)}), f32[16,17,1,128]{3,2,1,0:T(1,128)S(1)}, u32[]{:S(2)}, u32[]{:S(2)}) async-start(f32[16,17,1,128]{3,2,1,0:T(1,128)} %bitcast.4), calls=%async_computation | async-start | bytes 278528 | tf_op jit(solution)/shard_map/all_to_all | solution.py:240
  12.9 0.0 copy-done.4
  12.9 0.6 %collective-permute-start = (f32[16,512]{1,0:T(8,128)S(1)}, f32[16,512]{1,0:T(8,128)S(1)}, u32[]{:S(2)}, u32[]{:S(2)}) collective-permute-start(f32[16,512]{1,0:T(8,128)S(1)} %copy-done.4), channel_id=1, source_target_pairs={{0,16},{16,0},{1,17},{17,1},{2,18},{18,2},{3,19},{19,3},{4,20},{20... | collective-permute-start | bytes 98312 | tf_op jit(solution)/shard_map/ppermute | solution.py:262
  13.5 0.0 collective-permute-done.1.refs_0_
  13.6 0.0 copy-start.1
  13.6 0.0 copy-start
  13.6 3.3 %collective-permute-done.rhs_ref = f32[16,512]{1,0:T(8,128)S(1)} collective-permute-done((f32[16,512]{1,0:T(8,128)S(1)}, f32[16,512]{1,0:T(8,128)S(1)}, u32[]{:S(2)}, u32[]{:S(2)}) %collective-permute-start) | collective-permute-done | bytes 32800 | tf_op jit(solution)/shard_map/ppermute | solution.py:262
  16.9 0.4 %all-to-all-done = f32[16,17,1,128]{3,2,1,0:T(1,128)S(1)} async-done(((f32[16,17,1,128]{3,2,1,0:T(1,128)}), f32[16,17,1,128]{3,2,1,0:T(1,128)S(1)}, u32[]{:S(2)}, u32[]{:S(2)}) %all-to-all-start) | async-done | bytes 139296 | tf_op jit(solution)/shard_map/all_to_all | solution.py:240
  17.4 1.0 %last_section.1 = (f32[2,16,512]{2,1,0:T(8,128)S(1)}, f32[16,16,128]{2,1,0:T(8,128)}) custom-call(f32[272,128]{1,0:T(8,128)S(1)} %bitcast.3, f32[16,512]{1,0:T(8,128)S(1)} %collective-permute-done.rhs_ref, bf16[4,128,128]{2,1,0:T(8,128)(2,1)S(1)} %get-tuple-element.21.high_ref, bf16[4,128,128]{2,1,0:T(8,128)(2,1)S(1)} %get-tuple-element.22.low_ref), custom_call_target="tpu_custom_call" | custom-call | tf_op jit(solution)/shard_map/last_section/pallas_call | solution.py:267
  18.4 0.0 copy-start.2
  18.4 6.1 %all-to-all-start.1 = ((f32[16,16,128]{2,1,0:T(8,128)}), f32[16,16,128]{2,1,0:T(8,128)S(1)}, u32[]{:S(2)}, u32[]{:S(2)}) async-start(f32[16,16,128]{2,1,0:T(8,128)} %get-tuple-element.23), calls=%async_computation.1 | async-start | bytes 262144 | tf_op jit(solution)/shard_map/all_to_all | solution.py:240
  24.5 0.0 copy-start.3
  24.5 0.6 %collective-permute-start.2 = (f32[2,16,512]{2,1,0:T(8,128)S(1)}, f32[2,16,512]{2,1,0:T(8,128)S(1)}, u32[]{:S(2)}, u32[]{:S(2)}) collective-permute-start(f32[2,16,512]{2,1,0:T(8,128)S(1)} %get-tuple-element.29), channel_id=1, source_target_pairs={{0,16},{16,0},{1,17},{17,1},{2,18},{18,2},{3,19},{19,3},{4,20},{20... | collective-permute-start | bytes 196616 | tf_op jit(solution)/shard_map/ppermute | solution.py:281
  25.1 0.0 copy-done.1
  25.1 0.0 copy-done
  25.1 0.0 copy-done.2
  25.1 0.1 copy-done.3
  25.2 0.1 split_weights.2
  25.3 3.5 %collective-permute-done.2.rest_0_ = f32[2,16,512]{2,1,0:T(8,128)S(1)} collective-permute-done((f32[2,16,512]{2,1,0:T(8,128)S(1)}, f32[2,16,512]{2,1,0:T(8,128)S(1)}, u32[]{:S(2)}, u32[]{:S(2)}) %collective-permute-start.2) | collective-permute-done | bytes 65568 | tf_op jit(solution)/shard_map/ppermute | solution.py:281
  28.8 0.0 all-to-all-done.1.picked_ref
  28.9 1.2 %backward_last.1 = (f32[16,512]{1,0:T(8,128)}, f32[16,512]{1,0:T(8,128)}) custom-call(s32[8,128]{1,0:T(8,128)S(1)} %get-tuple-element.18.slots_ref, f32[16,16,128]{2,1,0:T(8,128)S(1)} %all-to-all-done.1.picked_ref, f32[16,512]{1,0:T(8,128)S(1)} %get-tuple-element.24.values_ref, bf16[4,128,128]{2,1,0:T(8,128)(2,1)S(1)} %get-tuple-element.25.inverse_high_ref, ...), custom_call_target="tpu_custom_call" | custom-call | tf_op jit(solution)/shard_map/backward_last/pallas_call | solution.py:282
  (1 shorter events, 0.0 us)
Async XLA Ops:
  0.6 12.9 %collective-permute-start.1 = (f32[4,128,128]{2,1,0:T(8,128)}, f32[4,128,128]{2,1,0:T(8,128)S(1)}, u32[]{:S(2)}, u32[]{:S(2)}) collective-permute-start(f32[4,128,128]{2,1,0:T(8,128)} %refs_2_.1), channel_id=1, source_target_pairs={{0,16},{16,0},{1,17},{17,1},{2,18},{18,2},{3,19},{19,3},{4,20},{20... | collective-permute-start | bytes 786440 | tf_op jit(solution)/shard_map/ppermute | solution.py:244
  5.8 7.2 %copy-start.4 = (f32[16,512]{1,0:T(8,128)S(1)}, f32[16,512]{1,0:T(8,128)}, u32[]{:S(2)}) copy-start(f32[16,512]{1,0:T(8,128)} %get-tuple-element.20) | copy-start | bytes 98308
  5.8 11.6 %all-to-all-start = ((f32[16,17,1,128]{3,2,1,0:T(1,128)}), f32[16,17,1,128]{3,2,1,0:T(1,128)S(1)}, u32[]{:S(2)}, u32[]{:S(2)}) async-start(f32[16,17,1,128]{3,2,1,0:T(1,128)} %bitcast.4), calls=%async_computation | async-start | bytes 278528 | tf_op jit(solution)/shard_map/all_to_all | solution.py:240
  12.9 4.0 %collective-permute-start = (f32[16,512]{1,0:T(8,128)S(1)}, f32[16,512]{1,0:T(8,128)S(1)}, u32[]{:S(2)}, u32[]{:S(2)}) collective-permute-start(f32[16,512]{1,0:T(8,128)S(1)} %copy-done.4), channel_id=1, source_target_pairs={{0,16},{16,0},{1,17},{17,1},{2,18},{18,2},{3,19},{19,3},{4,20},{20... | collective-permute-start | bytes 98312 | tf_op jit(solution)/shard_map/ppermute | solution.py:262
  13.6 11.6 %copy-start.1 = (f32[4,128,128]{2,1,0:T(8,128)S(1)}, f32[4,128,128]{2,1,0:T(8,128)}, u32[]{:S(2)}) copy-start(f32[4,128,128]{2,1,0:T(8,128)} %refs_2_.1) | copy-start | bytes 786436
  13.6 11.5 %copy-start = (f32[4,2,128,128]{3,2,1,0:T(8,128)S(1)}, f32[4,2,128,128]{3,2,1,0:T(8,128)}, u32[]{:S(2)}) copy-start(f32[4,2,128,128]{3,2,1,0:T(8,128)} %refs_3_.1) | copy-start | bytes 1572868
  18.4 6.7 %copy-start.2 = (f32[16,512]{1,0:T(8,128)S(1)}, f32[16,512]{1,0:T(8,128)}, u32[]{:S(2)}) copy-start(f32[16,512]{1,0:T(8,128)} %get-tuple-element.17.refs_1_) | copy-start | bytes 98308
  18.4 10.4 %all-to-all-start.1 = ((f32[16,16,128]{2,1,0:T(8,128)}), f32[16,16,128]{2,1,0:T(8,128)S(1)}, u32[]{:S(2)}, u32[]{:S(2)}) async-start(f32[16,16,128]{2,1,0:T(8,128)} %get-tuple-element.23), calls=%async_computation.1 | async-start | bytes 262144 | tf_op jit(solution)/shard_map/all_to_all | solution.py:240
  24.5 0.7 %copy-start.3 = (s32[8,128]{1,0:T(8,128)S(1)}, s32[8,128]{1,0:T(8,128)}, u32[]{:S(2)}) copy-start(s32[8,128]{1,0:T(8,128)} %get-tuple-element.16.refs_0_) | copy-start | bytes 12292
  24.5 4.3 %collective-permute-start.2 = (f32[2,16,512]{2,1,0:T(8,128)S(1)}, f32[2,16,512]{2,1,0:T(8,128)S(1)}, u32[]{:S(2)}, u32[]{:S(2)}) collective-permute-start(f32[2,16,512]{2,1,0:T(8,128)S(1)} %get-tuple-element.29), channel_id=1, source_target_pairs={{0,16},{16,0},{1,17},{17,1},{2,18},{18,2},{3,19},{19,3},{4,20},{20... | collective-permute-start | bytes 196616 | tf_op jit(solution)/shard_map/ppermute | solution.py:281

commit v4 on v3

--- a/solution.py
+++ b/solution.py
@@ -8,6 +8,8 @@
 from jax.sharding import PartitionSpec as P
 
 VMEM = pl.BlockSpec(memory_space=pltpu.VMEM)
+FIRST = 7
+SECOND = 11
 COVER = 20_000_000_000
 HBM = pl.BlockSpec(memory_space=pltpu.HBM)
 
@@ -85,54 +87,66 @@
 
 def place_answers(arrived_ref, answers_ref, solved, rhs_count):
     stride = rhs_count + 1
-    for column in range(answers_ref.shape[0]):
-        last = (column + 1) * stride
+    columns = answers_ref.shape[0]
+    for column in range(columns):
+        last = ((column ^ (FIRST % columns)) + 1) * stride
         row = arrived_ref[last - 1 : last, :]
         answer = jnp.zeros_like(solved[0])
         for local, values in enumerate(solved):
             answer = jnp.where(row == local, values, answer)
-        answers_ref[column] = answer
+        answers_ref[column ^ (SECOND % columns)] = answer
 
 
 def forward_kernel(targets_hbm, rhs_hbm, inverse_hbm, couplings_hbm, *rest):
-    *incoming_ref, values_ref, passed_ref, slots_ref, out_ref = rest[:-5]
+    *incoming_ref, values_ref, slots_ref, out_ref = rest[:-5]
     targets_ref, rhs_ref, inverse_ref, couplings_ref, sems = rest[-5:]
-    sources = (targets_hbm, rhs_hbm, inverse_hbm, couplings_hbm)
-    places = (targets_ref, rhs_ref, inverse_ref, couplings_ref)
-    copies = [
-        pltpu.make_async_copy(source, place, sems.at[i])
-        for i, (source, place) in enumerate(zip(sources, places))
-    ]
-    for copy in copies:
-        copy.start()
-    out_ref[...] = jnp.full(out_ref.shape, -1.0, jnp.float32)
     local_count, width, _ = inverse_ref.shape
     fanout = couplings_ref.shape[1]
     rhs_count = rhs_ref.shape[0]
     stride = rhs_count + 1
     columns = out_ref.shape[0] // stride
-    copies[1].wait()
-    copies[2].wait()
-    passed_ref[...] = rhs_ref[...]
-    solved = []
-    for local, lanes in enumerate(lane_blocks(width, local_count)):
-        source = rhs_ref[:, lanes]
-        if incoming_ref:
-            source = source - incoming_ref[0][:, lanes]
-        solved.append(times(source, split(inverse_ref[local])))
-        values_ref[:, lanes] = solved[local]
-    copies[0].wait()
-    copies[3].wait()
-    for local in range(local_count):
-        for k in range(fanout):
-            target = targets_ref[k, local]
-            slot = columns - 1 - target // local_count
-            start = slot * stride
-            row = jnp.full((1, width), target % local_count, jnp.int32)
-            out_ref[pl.ds(start, rhs_count), :] = times(solved[local], split(couplings_ref[local, k]))
-            out_ref[pl.ds(start + rhs_count, 1), :] = row.astype(jnp.float32)
-            pair = local * fanout + k
-            slots_ref[pair : pair + 1, :] = jnp.full((1, width), slot, jnp.int32)
+    has_targets = lax.axis_index("section") < lax.axis_size("section") - 1
+
+    @pl.when(has_targets)
+    def _():
+        sources = (targets_hbm, rhs_hbm, inverse_hbm, couplings_hbm)
+        places = (targets_ref, rhs_ref, inverse_ref, couplings_ref)
+        copies = [
+            pltpu.make_async_copy(source, place, sems.at[i])
+            for i, (source, place) in enumerate(zip(sources, places))
+        ]
+        for copy in copies:
+            copy.start()
+        out_ref[...] = jnp.full(out_ref.shape, -1.0, jnp.float32)
+        copies[1].wait()
+        copies[2].wait()
+        solved = []
+        for local, lanes in enumerate(lane_blocks(width, local_count)):
+            source = rhs_ref[:, lanes]
+            if incoming_ref:
+                source = source - incoming_ref[0][:, lanes]
+            solved.append(times(source, split(inverse_ref[local])))
+            values_ref[:, lanes] = solved[local]
+        copies[0].wait()
+        copies[3].wait()
+        for local in range(local_count):
+            for k in range(fanout):
+                target = targets_ref[k, local]
+                owner = target // local_count
+                start = (owner ^ (FIRST % columns)) * stride
+                product = times(solved[local], split(couplings_ref[local, k]))
+                row = jnp.full((1, width), target % local_count, jnp.int32)
+                out_ref[pl.ds(start, rhs_count), :] = product
+                out_ref[pl.ds(start + rhs_count, 1), :] = row.astype(jnp.float32)
+                slot = jnp.full((1, width), owner ^ (SECOND % columns), jnp.int32)
+                pair = local * fanout + k
+                slots_ref[pair : pair + 1, :] = slot
+
+    @pl.when(jnp.logical_not(has_targets))
+    def _():
+        out_ref[...] = jnp.full(out_ref.shape, -1.0, jnp.float32)
+        values_ref[...] = jnp.zeros(values_ref.shape, jnp.float32)
+        slots_ref[...] = jnp.zeros(slots_ref.shape, jnp.int32)
 
 
 def sum_kernel(arrived_ref, sums_ref):
@@ -142,17 +156,25 @@
         sums_ref[:, lanes[local]] = total
 
 
-def last_kernel(arrived_ref, rhs_ref, high_ref, low_ref, pair_ref, answers_ref):
+def solve_last(rhs_ref, sums, high_ref, low_ref):
+    local_count, width, _ = high_ref.shape
+    lanes = lane_blocks(width, local_count)
+    inverse = [(high_ref[i], low_ref[i]) for i in range(local_count)]
+    forward = [times(rhs_ref[:, lanes[i]] - sums[i], inverse[i]) for i in range(local_count)]
+    return forward, [times_transposed(forward[i], inverse[i]) for i in range(local_count)]
+
+
+def last_kernel(arrived_ref, rhs_ref, high_ref, low_ref, sums_ref, *rest):
+    *solved_ref, answers_ref = rest
     local_count, width, _ = high_ref.shape
     rhs_count = rhs_ref.shape[0]
     sums = summed_by_row(arrived_ref, local_count, rhs_count)
-    lanes = lane_blocks(width, local_count)
-    inverse = [(high_ref[i], low_ref[i]) for i in range(local_count)]
-    forward = [times(rhs_ref[:, lanes[i]] - sums[i], inverse[i]) for i in range(local_count)]
-    backward = [times_transposed(forward[i], inverse[i]) for i in range(local_count)]
-    for local in range(local_count):
-        pair_ref[0, :, lanes[local]] = forward[local]
-        pair_ref[1, :, lanes[local]] = backward[local]
+    for local, lanes in enumerate(lane_blocks(width, local_count)):
+        sums_ref[:, lanes] = sums[local]
+    _, backward = solve_last(rhs_ref, sums, high_ref, low_ref)
+    for ref in solved_ref:
+        for local, lanes in enumerate(lane_blocks(width, local_count)):
+            ref[:, lanes] = backward[local]
     place_answers(arrived_ref, answers_ref, backward, rhs_count)
 
 
@@ -172,9 +194,7 @@
     couplings_low_ref,
     *rest,
 ):
-    *pair_ref, solution_ref = rest
-    if pair_ref:
-        pair_ref, forward_ref = pair_ref
+    *last_refs, solution_ref = rest
     local_count, width, _ = inverse_high_ref.shape
     fanout = couplings_high_ref.shape[1]
     lanes = lane_blocks(width, local_count)
@@ -197,13 +217,17 @@
             inverse = (inverse_high_ref[local], inverse_low_ref[local])
             solution_ref[:, lanes[local]] = times_transposed(sources[local], inverse)
 
-    if not isinstance(pair_ref, list):
+    if last_refs:
+        rhs_ref, sums_ref, forward_ref = last_refs
         is_last = lax.axis_index("section") == lax.axis_size("section") - 1
 
         @pl.when(is_last)
         def _():
-            forward_ref[...] = pair_ref[0]
-            solution_ref[...] = pair_ref[1]
+            sums = [sums_ref[:, lane] for lane in lanes]
+            results = solve_last(rhs_ref, sums, inverse_high_ref, inverse_low_ref)
+            for local, lane in enumerate(lanes):
+                forward_ref[:, lane] = results[0][local]
+                solution_ref[:, lane] = results[1][local]
 
         @pl.when(jnp.logical_not(is_last))
         def _():
@@ -226,7 +250,6 @@
     flat = jax.ShapeDtypeStruct(rhs.shape, jnp.float32)
     slots = jax.ShapeDtypeStruct((columns * stride, width), jnp.float32)
     answered = jax.ShapeDtypeStruct((columns, rhs_count, width), jnp.float32)
-    pair = jax.ShapeDtypeStruct((2,) + rhs.shape, jnp.float32)
     owners = jax.ShapeDtypeStruct((local_count * couplings.shape[1], width), jnp.int32)
     aimed = targets.T
     inputs = (aimed, rhs, inverse_blocks, couplings)
@@ -234,53 +257,55 @@
     held += [pltpu.VMEM(a.shape, a.dtype) for a in inputs[1:]]
     held += [pltpu.SemaphoreType.DMA((len(inputs),))]
 
-    members = [list(range(columns))[::-1]]
-
-    def exchanged(value):
+
+    def exchanged(value, mask):
+        members = [[i ^ (mask % columns) for i in range(columns)]]
         return lax.all_to_all(
             value, "col", split_axis=0, concat_axis=0, tiled=True, axis_index_groups=members
         )
 
-    next_inverse = lax.ppermute(inverse_blocks, "section", down)
-
     incoming = ()
     for step in range(sections - 1):
-        values, passed, slot_rows, outgoing = kernel_call(
+        values, slot_rows, outgoing = kernel_call(
             forward_kernel,
-            (flat, flat, owners, slots),
+            (flat, owners, slots),
             [HBM] * len(inputs) + [VMEM] * len(incoming),
             "forward",
             scratch=held,
             vmem=60*2**20,
         )(*inputs, *incoming)
-        arrived = exchanged(outgoing.reshape(columns, stride, 1, width)).reshape(slots.shape)
+        if step == 0:
+            sent_inverse, sent_rhs, _ = lax.optimization_barrier((inverse_blocks, rhs, values))
+        arrived = exchanged(outgoing.reshape(columns, stride, 1, width), FIRST).reshape(slots.shape)
         if step < sections - 2:
             sums = kernel_call(sum_kernel, flat, [VMEM], "sum_rows")(arrived)
             moved = lax.ppermute(sums, "section", up)
             incoming = (jnp.where(my_section == 0, 0.0, moved),)
 
-    next_rhs = lax.ppermute(passed, "section", down)
+    next_inverse = lax.ppermute(sent_inverse, "section", down)
+    next_rhs = lax.ppermute(sent_rhs, "section", down)
     next_split = split_arrays((next_inverse,), COVER)
-    slot_rows, values, *weights = split_arrays(
-        (inverse_blocks, couplings), COVER, (slot_rows, values)
-    )
-    last, answers = kernel_call(last_kernel, (pair, answered), [VMEM] * 4, "last_section")(
+    slot_rows, values, own_rhs, *weights = split_arrays(
+        (inverse_blocks, couplings), COVER, (slot_rows, values, rhs)
+    )
+    last_shapes = (flat, flat, answered) if sections > 2 else (flat, answered)
+    sums, *last, answers = kernel_call(last_kernel, last_shapes, [VMEM] * 4, "last_section")(
         arrived, next_rhs, *next_split
     )
     for step in range(sections - 1):
-        picked = exchanged(answers)
+        picked = exchanged(answers, SECOND)
         operands = (slot_rows, picked, values, *weights)
         if step < sections - 2:
             solved = kernel_call(backward_kernel, flat, [VMEM] * len(operands), "backward")(
                 *operands
             )
             moved = lax.ppermute(solved, "section", down)
-            following = jnp.where(my_section == sections - 2, last[1], moved)
+            following = jnp.where(my_section == sections - 2, last[0], moved)
             answers = kernel_call(place_kernel, answered, [VMEM, VMEM], "place")(arrived, following)
 
-    final = lax.ppermute(last, "section", up)
-    return kernel_call(backward_kernel, (flat, flat), [VMEM] * (len(operands) + 1), "backward_last")(
-        *operands, final
+    operands += (own_rhs, lax.ppermute(sums, "section", up))
+    return kernel_call(backward_kernel, (flat, flat), [VMEM] * len(operands), "backward_last")(
+        *operands
     )
 
 

time: 30.4 us -> 27.6 us (0.908)
  waiting for transfers between devices: 7.3 us -> 5.2 us
  starting transfers between devices: 17.5 us -> 16.7 us
    ppermute x3, waiting for transfers between devices: 6.86 us -> 4.01 us  [the longest x1 2.05 us: body(): next_rhs = lax.ppermute(sent_rhs, 'section', down)]
    all_to_all x2, starting transfers between devices: 13.3 us -> 11.3 us  [exchanged(): lax.all_to_all(value, 'col', split_axis=0, concat_axis=0, tiled=True, axi...]
    ppermute x3, starting transfers between devices: 4.2 us -> 5.42 us  [the longest x1 1.88 us: body(): next_rhs = lax.ppermute(sent_rhs, 'section', down)]
    all_to_all x2, waiting for transfers between devices: 0.43 us -> 1.2 us  [exchanged(): lax.all_to_all(value, 'col', split_axis=0, concat_axis=0, tiled=True, axi...]
  transfers between devices with their start and end apart: 5 -> 5, of which waited for: 3 -> 3; matrix products, arithmetic and copies ran while one was open for 0% -> 0% of each run, Pallas kernels for 8% -> 1%
where the time goes in v4:
time: 27.6 us; the launch traced here: 27.2 us
  starting transfers between devices  16.7 us (61%)
  waiting for transfers between devices  5.2 us (19%)
  Pallas kernels  4.55 us (16%)
  between operations  0.68 us (2%)
    all_to_all x2, starting transfers between devices, exchanged(): lax.all_to_all(value, 'col', split_axis=0, concat_axis=0, tiled=True, axi...  11.3 us
    pallas_call x1, Pallas kernels, body(): kernel_call(forward_kernel, (flat, owners, slots), [HBM] * len(inputs) +...  2.19 us
    ppermute x1, waiting for transfers between devices, body(): next_rhs = lax.ppermute(sent_rhs, 'section', down)  2.05 us
    ppermute x1, waiting for transfers between devices, body(): operands += (own_rhs, lax.ppermute(sums, 'section', up))  1.96 us
    ppermute x1, starting transfers between devices, body(): next_rhs = lax.ppermute(sent_rhs, 'section', down)  1.88 us
    ppermute x1, starting transfers between devices, body(): operands += (own_rhs, lax.ppermute(sums, 'section', up))  1.81 us
    ppermute x1, starting transfers between devices, body(): next_inverse = lax.ppermute(sent_inverse, 'section', down)  1.72 us
    all_to_all x2, waiting for transfers between devices, exchanged(): lax.all_to_all(value, 'col', split_axis=0, concat_axis=0, tiled=True, axi...  1.2 us
  transfers between devices with their start and end apart: 5, of which 3 were waited for; matrix products, arithmetic and copies ran while one was open for 0% of the time, Pallas kernels for 1%

profile of v4, /device:TPU:0, one launch (start us, length us, event | category | flops | bytes accessed | tf_op | source)
XLA Modules:
  0.0 27.2 jit_solution(2988195379095832727)
XLA Ops:
  0.6 0.0 copy-start.1
  0.6 2.2 %forward.1 = (f32[16,512]{1,0:T(8,128)}, s32[8,128]{1,0:T(8,128)}, f32[272,128]{1,0:T(8,128)}) custom-call(s32[2,4]{1,0:T(2,128)} %bitcast.5, f32[16,512]{1,0:T(8,128)} %refs_2_.1, f32[4,128,128]{2,1,0:T(8,128)} %refs_3_.1, f32[4,2,128,128]{3,2,1,0:T(8,128)} %refs_4_.1), custom_call_target="tpu_custom_call" | custom-call | tf_op jit(solution)/shard_map/forward/pallas_call | solution.py:269
  2.8 0.0 copy-done.1
  2.8 1.7 %collective-permute-start.1 = (f32[4,128,128]{2,1,0:T(8,128)S(1)}, f32[4,128,128]{2,1,0:T(8,128)S(1)}, u32[]{:S(2)}, u32[]{:S(2)}) collective-permute-start(f32[4,128,128]{2,1,0:T(8,128)S(1)} %copy-done.1), channel_id=1, source_target_pairs={{0,16},{16,0},{1,17},{17,1},{2,18},{18,2},{3,19},{19,3},{4,20},{20... | collective-permute-start | bytes 786440 | tf_op jit(solution)/shard_map/ppermute | solution.py:285
  4.6 0.0 copy-start.2
  4.6 6.3 %all-to-all-start = ((f32[16,17,1,128]{3,2,1,0:T(1,128)}), f32[16,17,1,128]{3,2,1,0:T(1,128)S(1)}, u32[]{:S(2)}, u32[]{:S(2)}) async-start(f32[16,17,1,128]{3,2,1,0:T(1,128)} %bitcast.4), calls=%async_computation | async-start | bytes 278528 | tf_op jit(solution)/shard_map/all_to_all | solution.py:263
  10.9 0.0 copy-done.2
  10.9 1.9 %collective-permute-start = (f32[16,512]{1,0:T(8,128)S(1)}, f32[16,512]{1,0:T(8,128)S(1)}, u32[]{:S(2)}, u32[]{:S(2)}) collective-permute-start(f32[16,512]{1,0:T(8,128)S(1)} %copy-done.2), channel_id=1, source_target_pairs={{0,16},{16,0},{1,17},{17,1},{2,18},{18,2},{3,19},{19,3},{4,20},{20... | collective-permute-start | bytes 98312 | tf_op jit(solution)/shard_map/ppermute | solution.py:286
  12.8 0.0 collective-permute-done.1.refs_0_
  12.8 0.0 copy-start
  12.8 2.0 %collective-permute-done.rhs_ref = f32[16,512]{1,0:T(8,128)S(1)} collective-permute-done((f32[16,512]{1,0:T(8,128)S(1)}, f32[16,512]{1,0:T(8,128)S(1)}, u32[]{:S(2)}, u32[]{:S(2)}) %collective-permute-start) | collective-permute-done | bytes 32800 | tf_op jit(solution)/shard_map/ppermute | solution.py:286
  14.9 1.2 %all-to-all-done = f32[16,17,1,128]{3,2,1,0:T(1,128)S(1)} async-done(((f32[16,17,1,128]{3,2,1,0:T(1,128)}), f32[16,17,1,128]{3,2,1,0:T(1,128)S(1)}, u32[]{:S(2)}, u32[]{:S(2)}) %all-to-all-start) | async-done | bytes 139296 | tf_op jit(solution)/shard_map/all_to_all | solution.py:263
  16.0 1.0 %last_section.1 = (f32[16,512]{1,0:T(8,128)S(1)}, f32[16,16,128]{2,1,0:T(8,128)}) custom-call(f32[272,128]{1,0:T(8,128)S(1)} %bitcast.3, f32[16,512]{1,0:T(8,128)S(1)} %collective-permute-done.rhs_ref, bf16[4,128,128]{2,1,0:T(8,128)(2,1)S(1)} %get-tuple-element.24.high_ref, bf16[4,128,128]{2,1,0:T(8,128)(2,1)S(1)} %get-tuple-element.25.low_ref), custom_call_target="tpu_custom_call" | custom-call | tf_op jit(solution)/shard_map/last_section/pallas_call | solution.py:292
  17.1 0.0 copy-start.3
  17.1 0.0 copy-start.4
  17.1 5.0 %all-to-all-start.1 = ((f32[16,16,128]{2,1,0:T(8,128)}), f32[16,16,128]{2,1,0:T(8,128)S(1)}, u32[]{:S(2)}, u32[]{:S(2)}) async-start(f32[16,16,128]{2,1,0:T(8,128)} %get-tuple-element.26), calls=%async_computation.1 | async-start | bytes 262144 | tf_op jit(solution)/shard_map/all_to_all | solution.py:263
  22.1 1.8 %collective-permute-start.2 = (f32[16,512]{1,0:T(8,128)S(1)}, f32[16,512]{1,0:T(8,128)S(1)}, u32[]{:S(2)}, u32[]{:S(2)}) collective-permute-start(f32[16,512]{1,0:T(8,128)S(1)} %get-tuple-element.33), channel_id=1, source_target_pairs={{0,16},{16,0},{1,17},{17,1},{2,18},{18,2},{3,19},{19,3},{4,20},{20... | collective-permute-start | bytes 98312 | tf_op jit(solution)/shard_map/ppermute | solution.py:306
  23.9 0.0 copy-done
  23.9 0.0 copy-done.3
  23.9 0.0 copy-done.4
  23.9 0.1 split_weights.2
  24.1 2.0 %collective-permute-done.2.rest_1_ = f32[16,512]{1,0:T(8,128)S(1)} collective-permute-done((f32[16,512]{1,0:T(8,128)S(1)}, f32[16,512]{1,0:T(8,128)S(1)}, u32[]{:S(2)}, u32[]{:S(2)}) %collective-permute-start.2) | collective-permute-done | bytes 32800 | tf_op jit(solution)/shard_map/ppermute | solution.py:306
  26.0 0.0 all-to-all-done.1.picked_ref
  26.0 1.2 %backward_last.1 = (f32[16,512]{1,0:T(8,128)}, f32[16,512]{1,0:T(8,128)}) custom-call(s32[8,128]{1,0:T(8,128)S(1)} %get-tuple-element.20.slots_ref, f32[16,16,128]{2,1,0:T(8,128)S(1)} %all-to-all-done.1.picked_ref, f32[16,512]{1,0:T(8,128)S(1)} %get-tuple-element.27.values_ref, bf16[4,128,128]{2,1,0:T(8,128)(2,1)S(1)} %get-tuple-element.28.inverse_high_ref, ...), custom_call_target="tpu_custom_call" | custom-call | tf_op jit(solution)/shard_map/backward_last/pallas_call | solution.py:307
  (1 shorter events, 0.0 us)
Async XLA Ops:
  0.6 2.2 %copy-start.1 = (f32[4,128,128]{2,1,0:T(8,128)S(1)}, f32[4,128,128]{2,1,0:T(8,128)}, u32[]{:S(2)}) copy-start(f32[4,128,128]{2,1,0:T(8,128)} %refs_3_.1) | copy-start | bytes 786436
  2.8 9.9 %collective-permute-start.1 = (f32[4,128,128]{2,1,0:T(8,128)S(1)}, f32[4,128,128]{2,1,0:T(8,128)S(1)}, u32[]{:S(2)}, u32[]{:S(2)}) collective-permute-start(f32[4,128,128]{2,1,0:T(8,128)S(1)} %copy-done.1), channel_id=1, source_target_pairs={{0,16},{16,0},{1,17},{17,1},{2,18},{18,2},{3,19},{19,3},{4,20},{20... | collective-permute-start | bytes 786440 | tf_op jit(solution)/shard_map/ppermute | solution.py:285
  4.6 6.3 %copy-start.2 = (f32[16,512]{1,0:T(8,128)S(1)}, f32[16,512]{1,0:T(8,128)}, u32[]{:S(2)}) copy-start(f32[16,512]{1,0:T(8,128)} %refs_2_.1) | copy-start | bytes 98308
  4.6 11.5 %all-to-all-start = ((f32[16,17,1,128]{3,2,1,0:T(1,128)}), f32[16,17,1,128]{3,2,1,0:T(1,128)S(1)}, u32[]{:S(2)}, u32[]{:S(2)}) async-start(f32[16,17,1,128]{3,2,1,0:T(1,128)} %bitcast.4), calls=%async_computation | async-start | bytes 278528 | tf_op jit(solution)/shard_map/all_to_all | solution.py:263
  10.9 4.0 %collective-permute-start = (f32[16,512]{1,0:T(8,128)S(1)}, f32[16,512]{1,0:T(8,128)S(1)}, u32[]{:S(2)}, u32[]{:S(2)}) collective-permute-start(f32[16,512]{1,0:T(8,128)S(1)} %copy-done.2), channel_id=1, source_target_pairs={{0,16},{16,0},{1,17},{17,1},{2,18},{18,2},{3,19},{19,3},{4,20},{20... | collective-permute-start | bytes 98312 | tf_op jit(solution)/shard_map/ppermute | solution.py:286
  12.8 11.1 %copy-start = (f32[4,2,128,128]{3,2,1,0:T(8,128)S(1)}, f32[4,2,128,128]{3,2,1,0:T(8,128)}, u32[]{:S(2)}) copy-start(f32[4,2,128,128]{3,2,1,0:T(8,128)} %refs_4_.1) | copy-start | bytes 1572868
  17.1 6.8 %copy-start.3 = (f32[16,512]{1,0:T(8,128)S(1)}, f32[16,512]{1,0:T(8,128)}, u32[]{:S(2)}) copy-start(f32[16,512]{1,0:T(8,128)} %get-tuple-element.19.refs_1_) | copy-start | bytes 98308
  17.1 6.8 %copy-start.4 = (s32[8,128]{1,0:T(8,128)S(1)}, s32[8,128]{1,0:T(8,128)}, u32[]{:S(2)}) copy-start(s32[8,128]{1,0:T(8,128)} %get-tuple-element.18.refs_0_) | copy-start | bytes 12292
  17.1 8.9 %all-to-all-start.1 = ((f32[16,16,128]{2,1,0:T(8,128)}), f32[16,16,128]{2,1,0:T(8,128)S(1)}, u32[]{:S(2)}, u32[]{:S(2)}) async-start(f32[16,16,128]{2,1,0:T(8,128)} %get-tuple-element.26), calls=%async_computation.1 | async-start | bytes 262144 | tf_op jit(solution)/shard_map/all_to_all | solution.py:263
  22.1 3.9 %collective-permute-start.2 = (f32[16,512]{1,0:T(8,128)S(1)}, f32[16,512]{1,0:T(8,128)S(1)}, u32[]{:S(2)}, u32[]{:S(2)}) collective-permute-start(f32[16,512]{1,0:T(8,128)S(1)} %get-tuple-element.33), channel_id=1, source_target_pairs={{0,16},{16,0},{1,17},{17,1},{2,18},{18,2},{3,19},{19,3},{4,20},{20... | collective-permute-start | bytes 98312 | tf_op jit(solution)/shard_map/ppermute | solution.py:306

commit v5 on v4

--- a/solution.py
+++ b/solution.py
@@ -52,21 +52,39 @@
     )
 
 
-def split_kernel(count, kept, *refs):
-    passed, arrays, refs = refs[:kept], refs[kept : kept + count], refs[kept + count :]
-    for i in range(kept):
-        refs[i][...] = passed[i][...]
-    for i, array in enumerate(arrays):
-        at = kept + 2 * i
-        refs[at][...], refs[at + 1][...] = split(array[...])
-
-
-def split_arrays(arrays, flops, kept=()):
-    out = tuple(jax.ShapeDtypeStruct(a.shape, a.dtype) for a in kept)
-    out += tuple(jax.ShapeDtypeStruct(a.shape, jnp.bfloat16) for a in arrays for _ in range(2))
-    kernel = functools.partial(split_kernel, len(arrays), len(kept))
-    specs = [VMEM] * (len(kept) + len(arrays))
-    return kernel_call(kernel, out, specs, "split_weights", flops)(*kept, *arrays)
+def square_kernel(inverse_ref, high_ref, low_ref):
+    for local in range(inverse_ref.shape[0]):
+        inverse = inverse_ref[local]
+        high_ref[local], low_ref[local] = split(times_transposed(inverse, split(inverse)))
+
+
+def fold_kernel(
+    slots_ref,
+    values_ref,
+    rhs_ref,
+    inverse_ref,
+    couplings_ref,
+    slots_out,
+    values_out,
+    rhs_out,
+    base_ref,
+    inverse_high_ref,
+    inverse_low_ref,
+    high_ref,
+    low_ref,
+):
+    slots_out[...] = slots_ref[...]
+    values_out[...] = values_ref[...]
+    rhs_out[...] = rhs_ref[...]
+    local_count, fanout, width, _ = couplings_ref.shape
+    for local, lanes in enumerate(lane_blocks(width, local_count)):
+        inverse = inverse_ref[local]
+        parts = split(inverse)
+        inverse_high_ref[local], inverse_low_ref[local] = parts
+        base_ref[:, lanes] = times_transposed(values_ref[:, lanes], parts)
+        for k in range(fanout):
+            product = times(inverse, split(couplings_ref[local, k]))
+            high_ref[local, k], low_ref[local, k] = split(product)
 
 
 def lane_blocks(width, count):
@@ -171,7 +189,10 @@
     sums = summed_by_row(arrived_ref, local_count, rhs_count)
     for local, lanes in enumerate(lane_blocks(width, local_count)):
         sums_ref[:, lanes] = sums[local]
-    _, backward = solve_last(rhs_ref, sums, high_ref, low_ref)
+    backward = [
+        times(rhs_ref[:, lanes] - sums[i], (high_ref[i], low_ref[i]))
+        for i, lanes in enumerate(lane_blocks(width, local_count))
+    ]
     for ref in solved_ref:
         for local, lanes in enumerate(lane_blocks(width, local_count)):
             ref[:, lanes] = backward[local]
@@ -184,19 +205,9 @@
     place_answers(arrived_ref, answers_ref, [solved_ref[:, lane] for lane in lanes], rhs_count)
 
 
-def backward_kernel(
-    slots_ref,
-    picked_ref,
-    values_ref,
-    inverse_high_ref,
-    inverse_low_ref,
-    couplings_high_ref,
-    couplings_low_ref,
-    *rest,
-):
+def backward_kernel(slots_ref, picked_ref, base_ref, high_ref, low_ref, *rest):
     *last_refs, solution_ref = rest
-    local_count, width, _ = inverse_high_ref.shape
-    fanout = couplings_high_ref.shape[1]
+    local_count, fanout, width, _ = high_ref.shape
     lanes = lane_blocks(width, local_count)
 
     def solve():
@@ -206,19 +217,15 @@
             for pair in range(local_count * fanout):
                 chosen = slots_ref[pair : pair + 1, :] == column
                 blocks[pair] = jnp.where(chosen, block, blocks[pair])
-        sources = []
         for local in range(local_count):
-            source = values_ref[:, lanes[local]]
+            total = base_ref[:, lanes[local]]
             for k in range(fanout):
-                coupling = (couplings_high_ref[local, k], couplings_low_ref[local, k])
-                source = source - times_transposed(blocks[local * fanout + k], coupling)
-            sources.append(source)
-        for local in range(local_count):
-            inverse = (inverse_high_ref[local], inverse_low_ref[local])
-            solution_ref[:, lanes[local]] = times_transposed(sources[local], inverse)
+                folded = (high_ref[local, k], low_ref[local, k])
+                total = total - times_transposed(blocks[local * fanout + k], folded)
+            solution_ref[:, lanes[local]] = total
 
     if last_refs:
-        rhs_ref, sums_ref, forward_ref = last_refs
+        values_ref, rhs_ref, sums_ref, inverse_high_ref, inverse_low_ref, forward_ref = last_refs
         is_last = lax.axis_index("section") == lax.axis_size("section") - 1
 
         @pl.when(is_last)
@@ -284,17 +291,26 @@
 
     next_inverse = lax.ppermute(sent_inverse, "section", down)
     next_rhs = lax.ppermute(sent_rhs, "section", down)
-    next_split = split_arrays((next_inverse,), COVER)
-    slot_rows, values, own_rhs, *weights = split_arrays(
-        (inverse_blocks, couplings), COVER, (slot_rows, values, rhs)
-    )
+    def halves(array):
+        return (jax.ShapeDtypeStruct(array.shape, jnp.bfloat16),) * 2
+
+    next_square = kernel_call(square_kernel, halves(inverse_blocks), [VMEM], "square", COVER)(
+        next_inverse
+    )
+    slot_rows, values, own_rhs, base, *own_inverse, high, low = kernel_call(
+        fold_kernel,
+        (owners, flat, flat, flat, *halves(inverse_blocks), *halves(couplings)),
+        [VMEM] * 5,
+        "fold",
+        COVER,
+    )(slot_rows, values, rhs, inverse_blocks, couplings)
     last_shapes = (flat, flat, answered) if sections > 2 else (flat, answered)
     sums, *last, answers = kernel_call(last_kernel, last_shapes, [VMEM] * 4, "last_section")(
-        arrived, next_rhs, *next_split
+        arrived, next_rhs, *next_square
     )
     for step in range(sections - 1):
         picked = exchanged(answers, SECOND)
-        operands = (slot_rows, picked, values, *weights)
+        operands = (slot_rows, picked, base, high, low)
         if step < sections - 2:
             solved = kernel_call(backward_kernel, flat, [VMEM] * len(operands), "backward")(
                 *operands
@@ -303,7 +319,7 @@
             following = jnp.where(my_section == sections - 2, last[0], moved)
             answers = kernel_call(place_kernel, answered, [VMEM, VMEM], "place")(arrived, following)
 
-    operands += (own_rhs, lax.ppermute(sums, "section", up))
+    operands += (values, own_rhs, lax.ppermute(sums, "section", up), *own_inverse)
     return kernel_call(backward_kernel, (flat, flat), [VMEM] * len(operands), "backward_last")(
         *operands
     )

time: 27.6 us -> 27.3 us (0.989)
  waiting for transfers between devices: 5.2 us -> 4.52 us
  Pallas kernels: 4.55 us -> 4.93 us
    pallas_call x2, Pallas kernels: 0.16 us -> 0.84 us  [the longest x1 0.54 us: body(): kernel_call(fold_kernel, (owners, flat, flat, flat, *halves(inverse_block...]
    ppermute x1, waiting for transfers between devices: 1.96 us -> 1.54 us  [body(): lax.ppermute(sums, 'section', up)]
  transfers between devices with their start and end apart: 5 -> 5, of which waited for: 3 -> 3; matrix products, arithmetic and copies ran while one was open for 0% -> 0% of each run, Pallas kernels for 1% -> 3%
where the time goes in v5:
time: 27.3 us; the launch traced here: 26.9 us
  starting transfers between devices  16.7 us (61%)
  Pallas kernels  4.93 us (18%)
  waiting for transfers between devices  4.52 us (17%)
  between operations  0.69 us (3%)
    all_to_all x2, starting transfers between devices, exchanged(): lax.all_to_all(value, 'col', split_axis=0, concat_axis=0, tiled=True, axi...  11.3 us
    pallas_call x1, Pallas kernels, body(): kernel_call(forward_kernel, (flat, owners, slots), [HBM] * len(inputs) +...  2.19 us
    ppermute x1, starting transfers between devices, body(): next_rhs = lax.ppermute(sent_rhs, 'section', down)  1.88 us
    ppermute x1, starting transfers between devices, body(): lax.ppermute(sums, 'section', up)  1.81 us
    ppermute x1, waiting for transfers between devices, body(): next_rhs = lax.ppermute(sent_rhs, 'section', down)  1.78 us
    ppermute x1, starting transfers between devices, body(): next_inverse = lax.ppermute(sent_inverse, 'section', down)  1.72 us
    ppermute x1, waiting for transfers between devices, body(): lax.ppermute(sums, 'section', up)  1.54 us
    all_to_all x2, waiting for transfers between devices, exchanged(): lax.all_to_all(value, 'col', split_axis=0, concat_axis=0, tiled=True, axi...  1.2 us
  transfers between devices with their start and end apart: 5, of which 3 were waited for; matrix products, arithmetic and copies ran while one was open for 0% of the time, Pallas kernels for 3%

profile of v5, /device:TPU:0, one launch (start us, length us, event | category | flops | bytes accessed | tf_op | source)
XLA Modules:
  0.0 26.9 jit_solution(4758479141859729373)
XLA Ops:
  0.6 0.0 copy-start.1
  0.6 2.2 %forward.1 = (f32[16,512]{1,0:T(8,128)}, s32[8,128]{1,0:T(8,128)}, f32[272,128]{1,0:T(8,128)}) custom-call(s32[2,4]{1,0:T(2,128)} %bitcast.5, f32[16,512]{1,0:T(8,128)} %rhs_ref.1, f32[4,128,128]{2,1,0:T(8,128)} %inverse_ref.1, f32[4,2,128,128]{3,2,1,0:T(8,128)} %couplings_ref.1), custom_call_target="tpu_custom_call" | custom-call | tf_op jit(solution)/shard_map/forward/pallas_call | solution.py:276
  2.8 0.0 copy-done.1
  2.8 1.7 %collective-permute-start.1 = (f32[4,128,128]{2,1,0:T(8,128)S(1)}, f32[4,128,128]{2,1,0:T(8,128)S(1)}, u32[]{:S(2)}, u32[]{:S(2)}) collective-permute-start(f32[4,128,128]{2,1,0:T(8,128)S(1)} %copy-done.1), channel_id=1, source_target_pairs={{0,16},{16,0},{1,17},{17,1},{2,18},{18,2},{3,19},{19,3},{4,20},{20... | collective-permute-start | bytes 786440 | tf_op jit(solution)/shard_map/ppermute | solution.py:292
  4.6 0.0 copy-start.2
  4.6 6.3 %all-to-all-start = ((f32[16,17,1,128]{3,2,1,0:T(1,128)}), f32[16,17,1,128]{3,2,1,0:T(1,128)S(1)}, u32[]{:S(2)}, u32[]{:S(2)}) async-start(f32[16,17,1,128]{3,2,1,0:T(1,128)} %bitcast.4), calls=%async_computation | async-start | bytes 278528 | tf_op jit(solution)/shard_map/all_to_all | solution.py:270
  10.9 0.0 copy-done.2
  10.9 1.9 %collective-permute-start = (f32[16,512]{1,0:T(8,128)S(1)}, f32[16,512]{1,0:T(8,128)S(1)}, u32[]{:S(2)}, u32[]{:S(2)}) collective-permute-start(f32[16,512]{1,0:T(8,128)S(1)} %copy-done.2), channel_id=1, source_target_pairs={{0,16},{16,0},{1,17},{17,1},{2,18},{18,2},{3,19},{19,3},{4,20},{20... | collective-permute-start | bytes 98312 | tf_op jit(solution)/shard_map/ppermute | solution.py:293
  12.8 0.0 collective-permute-done.1.inverse_ref
  12.8 0.3 %square.1 = (bf16[4,128,128]{2,1,0:T(8,128)(2,1)S(1)}, bf16[4,128,128]{2,1,0:T(8,128)(2,1)S(1)}) custom-call(f32[4,128,128]{2,1,0:T(8,128)S(1)} %collective-permute-done.1.inverse_ref), custom_call_target="tpu_custom_call" | custom-call | flops 20000000000 | tf_op jit(solution)/shard_map/square/pallas_call | solution.py:297
  13.1 0.0 copy-start
  13.1 1.8 %collective-permute-done.rhs_ref = f32[16,512]{1,0:T(8,128)S(1)} collective-permute-done((f32[16,512]{1,0:T(8,128)S(1)}, f32[16,512]{1,0:T(8,128)S(1)}, u32[]{:S(2)}, u32[]{:S(2)}) %collective-permute-start) | collective-permute-done | bytes 32800 | tf_op jit(solution)/shard_map/ppermute | solution.py:293
  14.9 1.2 %all-to-all-done = f32[16,17,1,128]{3,2,1,0:T(1,128)S(1)} async-done(((f32[16,17,1,128]{3,2,1,0:T(1,128)}), f32[16,17,1,128]{3,2,1,0:T(1,128)S(1)}, u32[]{:S(2)}, u32[]{:S(2)}) %all-to-all-start) | async-done | bytes 139296 | tf_op jit(solution)/shard_map/all_to_all | solution.py:270
  16.0 0.9 %last_section.1 = (f32[16,512]{1,0:T(8,128)S(1)}, f32[16,16,128]{2,1,0:T(8,128)}) custom-call(f32[272,128]{1,0:T(8,128)S(1)} %bitcast.3, f32[16,512]{1,0:T(8,128)S(1)} %collective-permute-done.rhs_ref, bf16[4,128,128]{2,1,0:T(8,128)(2,1)S(1)} %get-tuple-element.25.high_ref, bf16[4,128,128]{2,1,0:T(8,128)(2,1)S(1)} %get-tuple-element.26.low_ref), custom_call_target="tpu_custom_call" | custom-call | tf_op jit(solution)/shard_map/last_section/pallas_call | solution.py:308
  16.9 0.0 copy-start.3
  16.9 0.0 copy-start.4
  16.9 5.0 %all-to-all-start.1 = ((f32[16,16,128]{2,1,0:T(8,128)}), f32[16,16,128]{2,1,0:T(8,128)S(1)}, u32[]{:S(2)}, u32[]{:S(2)}) async-start(f32[16,16,128]{2,1,0:T(8,128)} %get-tuple-element.27), calls=%async_computation.1 | async-start | bytes 262144 | tf_op jit(solution)/shard_map/all_to_all | solution.py:270
  22.0 1.8 %collective-permute-start.2 = (f32[16,512]{1,0:T(8,128)S(1)}, f32[16,512]{1,0:T(8,128)S(1)}, u32[]{:S(2)}, u32[]{:S(2)}) collective-permute-start(f32[16,512]{1,0:T(8,128)S(1)} %get-tuple-element.33), channel_id=1, source_target_pairs={{0,16},{16,0},{1,17},{17,1},{2,18},{18,2},{3,19},{19,3},{4,20},{20... | collective-permute-start | bytes 98312 | tf_op jit(solution)/shard_map/ppermute | solution.py:322
  23.8 0.0 copy-done
  23.8 0.0 copy-done.3
  23.8 0.0 copy-done.4
  23.8 0.5 %fold.1 = (s32[8,128]{1,0:T(8,128)S(1)}, f32[16,512]{1,0:T(8,128)S(1)}, f32[16,512]{1,0:T(8,128)S(1)}, f32[16,512]{1,0:T(8,128)S(1)}, bf16[4,128,128]{2,1,0:T(8,...) custom-call(s32[8,128]{1,0:T(8,128)S(1)} %copy-done.4, ...), custom_call_target="tpu_custom_call" | custom-call | flops 20000000000 | tf_op jit(solution)/shard_map/fold/pallas_call | solution.py:300
  24.3 1.5 %collective-permute-done.2.rest_2_ = f32[16,512]{1,0:T(8,128)S(1)} collective-permute-done((f32[16,512]{1,0:T(8,128)S(1)}, f32[16,512]{1,0:T(8,128)S(1)}, u32[]{:S(2)}, u32[]{:S(2)}) %collective-permute-start.2) | collective-permute-done | bytes 32800 | tf_op jit(solution)/shard_map/ppermute | solution.py:322
  25.9 0.0 all-to-all-done.1.picked_ref
  25.9 1.0 %backward_last.1 = (f32[16,512]{1,0:T(8,128)}, f32[16,512]{1,0:T(8,128)}) custom-call(s32[8,128]{1,0:T(8,128)S(1)} %get-tuple-element.21.slots_ref, f32[16,16,128]{2,1,0:T(8,128)S(1)} %all-to-all-done.1.picked_ref, f32[16,512]{1,0:T(8,128)S(1)} %get-tuple-element.28.base_ref, bf16[4,2,128,128]{3,2,1,0:T(8,128)(2,1)S(1)} %get-tuple-element.29.high_ref, ...), custom_call_target="tpu_custom_call" | custom-call | tf_op jit(solution)/shard_map/backward_last/pallas_call | solution.py:323
Async XLA Ops:
  0.6 2.2 %copy-start.1 = (f32[4,128,128]{2,1,0:T(8,128)S(1)}, f32[4,128,128]{2,1,0:T(8,128)}, u32[]{:S(2)}) copy-start(f32[4,128,128]{2,1,0:T(8,128)} %inverse_ref.1) | copy-start | bytes 786436
  2.8 9.9 %collective-permute-start.1 = (f32[4,128,128]{2,1,0:T(8,128)S(1)}, f32[4,128,128]{2,1,0:T(8,128)S(1)}, u32[]{:S(2)}, u32[]{:S(2)}) collective-permute-start(f32[4,128,128]{2,1,0:T(8,128)S(1)} %copy-done.1), channel_id=1, source_target_pairs={{0,16},{16,0},{1,17},{17,1},{2,18},{18,2},{3,19},{19,3},{4,20},{20... | collective-permute-start | bytes 786440 | tf_op jit(solution)/shard_map/ppermute | solution.py:292
  4.6 6.3 %copy-start.2 = (f32[16,512]{1,0:T(8,128)S(1)}, f32[16,512]{1,0:T(8,128)}, u32[]{:S(2)}) copy-start(f32[16,512]{1,0:T(8,128)} %rhs_ref.1) | copy-start | bytes 98308
  4.6 11.5 %all-to-all-start = ((f32[16,17,1,128]{3,2,1,0:T(1,128)}), f32[16,17,1,128]{3,2,1,0:T(1,128)S(1)}, u32[]{:S(2)}, u32[]{:S(2)}) async-start(f32[16,17,1,128]{3,2,1,0:T(1,128)} %bitcast.4), calls=%async_computation | async-start | bytes 278528 | tf_op jit(solution)/shard_map/all_to_all | solution.py:270
  10.9 4.0 %collective-permute-start = (f32[16,512]{1,0:T(8,128)S(1)}, f32[16,512]{1,0:T(8,128)S(1)}, u32[]{:S(2)}, u32[]{:S(2)}) collective-permute-start(f32[16,512]{1,0:T(8,128)S(1)} %copy-done.2), channel_id=1, source_target_pairs={{0,16},{16,0},{1,17},{17,1},{2,18},{18,2},{3,19},{19,3},{4,20},{20... | collective-permute-start | bytes 98312 | tf_op jit(solution)/shard_map/ppermute | solution.py:293
  13.1 10.7 %copy-start = (f32[4,2,128,128]{3,2,1,0:T(8,128)S(1)}, f32[4,2,128,128]{3,2,1,0:T(8,128)}, u32[]{:S(2)}) copy-start(f32[4,2,128,128]{3,2,1,0:T(8,128)} %couplings_ref.1) | copy-start | bytes 1572868
  16.9 6.8 %copy-start.3 = (f32[16,512]{1,0:T(8,128)S(1)}, f32[16,512]{1,0:T(8,128)}, u32[]{:S(2)}) copy-start(f32[16,512]{1,0:T(8,128)} %get-tuple-element.20.values_ref) | copy-start | bytes 98308
  16.9 6.8 %copy-start.4 = (s32[8,128]{1,0:T(8,128)S(1)}, s32[8,128]{1,0:T(8,128)}, u32[]{:S(2)}) copy-start(s32[8,128]{1,0:T(8,128)} %get-tuple-element.19.slots_ref) | copy-start | bytes 12292
  16.9 8.9 %all-to-all-start.1 = ((f32[16,16,128]{2,1,0:T(8,128)}), f32[16,16,128]{2,1,0:T(8,128)S(1)}, u32[]{:S(2)}, u32[]{:S(2)}) async-start(f32[16,16,128]{2,1,0:T(8,128)} %get-tuple-element.27), calls=%async_computation.1 | async-start | bytes 262144 | tf_op jit(solution)/shard_map/all_to_all | solution.py:270
  22.0 3.9 %collective-permute-start.2 = (f32[16,512]{1,0:T(8,128)S(1)}, f32[16,512]{1,0:T(8,128)S(1)}, u32[]{:S(2)}, u32[]{:S(2)}) collective-permute-start(f32[16,512]{1,0:T(8,128)S(1)} %get-tuple-element.33), channel_id=1, source_target_pairs={{0,16},{16,0},{1,17},{17,1},{2,18},{18,2},{3,19},{19,3},{4,20},{20... | collective-permute-start | bytes 98312 | tf_op jit(solution)/shard_map/ppermute | solution.py:322

commit v6 on v5

--- a/solution.py
+++ b/solution.py
@@ -8,8 +8,27 @@
 from jax.sharding import PartitionSpec as P
 
 VMEM = pl.BlockSpec(memory_space=pltpu.VMEM)
-FIRST = 7
-SECOND = 11
+FIRST = [11, 10, 15, 14, 7, 6, 3, 2, 9, 8, 13, 12, 5, 4, 1, 0]
+SECOND = [11, 10, 9, 8, 15, 14, 13, 12, 3, 2, 1, 0, 7, 6, 5, 4]
+
+
+def member_order(order, columns):
+    if columns == len(order):
+        return order
+    return [(columns * 11 // 16 - i) % columns for i in range(columns)]
+
+
+def slot_of(owner, order, columns):
+    if columns != len(order):
+        return (columns * 11 // 16 + columns - owner) % columns
+    low, high = (
+        sum(order.index(half + i) << (4 * i) for i in range(8)) for half in (0, 8)
+    )
+    low, high = (jnp.int32(v - (1 << 32) if v >= 1 << 31 else v) for v in (low, high))
+    packed = jnp.where(owner < 8, low, high)
+    return lax.shift_right_logical(packed, (owner % 8) * 4) & 15
+
+
 COVER = 20_000_000_000
 HBM = pl.BlockSpec(memory_space=pltpu.HBM)
 
@@ -36,7 +55,7 @@
     return times(left, right, 1)
 
 
-def kernel_call(kernel, out_shape, specs, name, flops=None, scratch=(), vmem=16 * 2**20):
+def kernel_call(kernel, out_shape, specs, name, flops=None, scratch=(), vmem=16 * 2**20, **kwargs):
     cost = None
     if flops is not None:
         cost = pl.CostEstimate(flops=flops, bytes_accessed=0, transcendentals=0)
@@ -44,7 +63,8 @@
         kernel,
         out_shape=out_shape,
         in_specs=specs,
-        out_specs=jax.tree.map(lambda _: VMEM, out_shape),
+        out_specs=kwargs.get("out_specs", jax.tree.map(lambda _: VMEM, out_shape)),
+        input_output_aliases=kwargs.get("aliases", {}),
         compiler_params=pltpu.CompilerParams(vmem_limit_bytes=vmem),
         cost_estimate=cost,
         scratch_shapes=scratch,
@@ -106,13 +126,15 @@
 def place_answers(arrived_ref, answers_ref, solved, rhs_count):
     stride = rhs_count + 1
     columns = answers_ref.shape[0]
+    first = member_order(FIRST, columns)
+    second = member_order(SECOND, columns)
     for column in range(columns):
-        last = ((column ^ (FIRST % columns)) + 1) * stride
+        last = (first.index(column) + 1) * stride
         row = arrived_ref[last - 1 : last, :]
         answer = jnp.zeros_like(solved[0])
         for local, values in enumerate(solved):
             answer = jnp.where(row == local, values, answer)
-        answers_ref[column ^ (SECOND % columns)] = answer
+        answers_ref[second.index(column)] = answer
 
 
 def forward_kernel(targets_hbm, rhs_hbm, inverse_hbm, couplings_hbm, *rest):
@@ -151,12 +173,12 @@
             for k in range(fanout):
                 target = targets_ref[k, local]
                 owner = target // local_count
-                start = (owner ^ (FIRST % columns)) * stride
+                start = slot_of(owner, FIRST, columns) * stride
                 product = times(solved[local], split(couplings_ref[local, k]))
                 row = jnp.full((1, width), target % local_count, jnp.int32)
                 out_ref[pl.ds(start, rhs_count), :] = product
                 out_ref[pl.ds(start + rhs_count, 1), :] = row.astype(jnp.float32)
-                slot = jnp.full((1, width), owner ^ (SECOND % columns), jnp.int32)
+                slot = jnp.full((1, width), slot_of(owner, SECOND, columns), jnp.int32)
                 pair = local * fanout + k
                 slots_ref[pair : pair + 1, :] = slot
 
@@ -206,7 +228,7 @@
 
 
 def backward_kernel(slots_ref, picked_ref, base_ref, high_ref, low_ref, *rest):
-    *last_refs, solution_ref = rest
+    *last_refs, solution_ref = rest if len(rest) == 1 else (*rest[:3], rest[4], rest[3])
     local_count, fanout, width, _ = high_ref.shape
     lanes = lane_blocks(width, local_count)
 
@@ -224,25 +246,45 @@
                 total = total - times_transposed(blocks[local * fanout + k], folded)
             solution_ref[:, lanes[local]] = total
 
-    if last_refs:
-        values_ref, rhs_ref, sums_ref, inverse_high_ref, inverse_low_ref, forward_ref = last_refs
-        is_last = lax.axis_index("section") == lax.axis_size("section") - 1
-
-        @pl.when(is_last)
-        def _():
-            sums = [sums_ref[:, lane] for lane in lanes]
-            results = solve_last(rhs_ref, sums, inverse_high_ref, inverse_low_ref)
-            for local, lane in enumerate(lanes):
-                forward_ref[:, lane] = results[0][local]
-                solution_ref[:, lane] = results[1][local]
-
-        @pl.when(jnp.logical_not(is_last))
-        def _():
-            forward_ref[...] = values_ref[...]
-            solve()
-
-    else:
+    if not last_refs:
         solve()
+        return
+
+    values_ref, forward_out, solution_out, sems = last_refs
+    section_is_last = lax.axis_index("section") == lax.axis_size("section") - 1
+
+    @pl.when(jnp.logical_not(section_is_last))
+    def _():
+        first = pltpu.make_async_copy(values_ref, forward_out, sems.at[0])
+        second = pltpu.make_async_copy(solution_ref, solution_out, sems.at[1])
+        first.start()
+        solve()
+        second.start()
+        first.wait()
+        second.wait()
+
+
+def finish_kernel(rhs_ref, sums_ref, high_ref, low_ref, *rest):
+    _, _, forward_out, solution_out, forward_ref, solution_ref, sems = rest
+    section_is_last = lax.axis_index("section") == lax.axis_size("section") - 1
+
+    @pl.when(section_is_last)
+    def _():
+        local_count, width, _ = high_ref.shape
+        lanes = lane_blocks(width, local_count)
+        sums = [sums_ref[:, lane] for lane in lanes]
+        forward, backward = solve_last(rhs_ref, sums, high_ref, low_ref)
+        for local, lane in enumerate(lanes):
+            forward_ref[:, lane] = forward[local]
+            solution_ref[:, lane] = backward[local]
+        copies = [
+            pltpu.make_async_copy(forward_ref, forward_out, sems.at[0]),
+            pltpu.make_async_copy(solution_ref, solution_out, sems.at[1]),
+        ]
+        for copy in copies:
+            copy.start()
+        for copy in copies:
+            copy.wait()
 
 
 def body(rhs, inverse_blocks, couplings, targets):
@@ -265,8 +307,8 @@
     held += [pltpu.SemaphoreType.DMA((len(inputs),))]
 
 
-    def exchanged(value, mask):
-        members = [[i ^ (mask % columns) for i in range(columns)]]
+    def exchanged(value, order):
+        members = [member_order(order, columns)]
         return lax.all_to_all(
             value, "col", split_axis=0, concat_axis=0, tiled=True, axis_index_groups=members
         )
@@ -319,10 +361,26 @@
             following = jnp.where(my_section == sections - 2, last[0], moved)
             answers = kernel_call(place_kernel, answered, [VMEM, VMEM], "place")(arrived, following)
 
-    operands += (values, own_rhs, lax.ppermute(sums, "section", up), *own_inverse)
-    return kernel_call(backward_kernel, (flat, flat), [VMEM] * len(operands), "backward_last")(
-        *operands
-    )
+    staged = pltpu.VMEM(flat.shape, flat.dtype)
+    sems = pltpu.SemaphoreType.DMA((2,))
+    results = kernel_call(
+        backward_kernel,
+        (flat, flat),
+        [VMEM] * (len(operands) + 1),
+        "backward_last",
+        scratch=[staged, sems],
+        out_specs=(HBM, HBM),
+    )(*operands, values)
+    received = lax.ppermute(sums, "section", up)
+    return kernel_call(
+        finish_kernel,
+        (flat, flat),
+        [VMEM] * 4 + [HBM] * 2,
+        "finish_last",
+        scratch=[staged, staged, sems],
+        out_specs=(HBM, HBM),
+        aliases={4: 0, 5: 1},
+    )(own_rhs, received, *own_inverse, *results)
 
 
 def solution(mesh):

time: 27.3 us -> 26.5 us (0.971)
  the two profiles are of different devices: /device:TPU:0 before, /device:TPU:1 now
where the time goes in v6:
time: 26.5 us; the launch traced here: 26.1 us
  starting transfers between devices  16 us (60%)
  Pallas kernels  4.95 us (19%)
  waiting for transfers between devices  4.44 us (17%)
  between operations  0.7 us (3%)
    all_to_all x2, starting transfers between devices, exchanged(): lax.all_to_all(value, 'col', split_axis=0, concat_axis=0, tiled=True, axi...  12 us
    all_to_all x2, waiting for transfers between devices, exchanged(): lax.all_to_all(value, 'col', split_axis=0, concat_axis=0, tiled=True, axi...  3.15 us
    pallas_call x1, Pallas kernels, body(): kernel_call(forward_kernel, (flat, owners, slots), [HBM] * len(inputs) +...  2.18 us
    ppermute x1, starting transfers between devices, body(): next_rhs = lax.ppermute(sent_rhs, 'section', down)  1.6 us
    ppermute x1, starting transfers between devices, body(): received = lax.ppermute(sums, 'section', up)  1.53 us
    ppermute x1, waiting for transfers between devices, body(): next_rhs = lax.ppermute(sent_rhs, 'section', down)  1.28 us
    pallas_call x1, Pallas kernels, body(): kernel_call(backward_kernel, (flat, flat), [VMEM] * (len(operands) + 1),...  1.02 us
    pallas_call x1, Pallas kernels, body(): kernel_call(last_kernel, last_shapes, [VMEM] * 4, 'last_section')  0.87 us
  transfers between devices with their start and end apart: 5, of which 3 were waited for; matrix products, arithmetic and copies ran while one was open for 0% of the time, Pallas kernels for 7%

profile of v6, /device:TPU:1, one launch (start us, length us, event | category | flops | bytes accessed | tf_op | source)
XLA Modules:
  0.0 26.1 jit_solution(11897189476212348022)
XLA Ops:
  0.6 0.0 copy-start.1
  0.6 2.2 %forward.1 = (f32[16,512]{1,0:T(8,128)}, s32[8,128]{1,0:T(8,128)}, f32[272,128]{1,0:T(8,128)}) custom-call(s32[2,4]{1,0:T(2,128)} %bitcast.5, f32[16,512]{1,0:T(8,128)} %rhs_ref.1, f32[4,128,128]{2,1,0:T(8,128)} %inverse_ref.1, f32[4,2,128,128]{3,2,1,0:T(8,128)} %couplings_ref.1), custom_call_target="tpu_custom_call" | custom-call | tf_op jit(solution)/shard_map/forward/pallas_call | solution.py:318
  2.8 0.0 copy-done.1
  2.8 0.8 %collective-permute-start.1 = (f32[4,128,128]{2,1,0:T(8,128)S(1)}, f32[4,128,128]{2,1,0:T(8,128)S(1)}, u32[]{:S(2)}, u32[]{:S(2)}) collective-permute-start(f32[4,128,128]{2,1,0:T(8,128)S(1)} %copy-done.1), channel_id=1, source_target_pairs={{0,16},{16,0},{1,17},{17,1},{2,18},{18,2},{3,19},{19,3},{4,20},{20... | collective-permute-start | bytes 786440 | tf_op jit(solution)/shard_map/ppermute | solution.py:334
  3.7 0.0 copy-start.2
  3.7 6.8 %all-to-all-start = ((f32[16,17,1,128]{3,2,1,0:T(1,128)}), f32[16,17,1,128]{3,2,1,0:T(1,128)S(1)}, u32[]{:S(2)}, u32[]{:S(2)}) async-start(f32[16,17,1,128]{3,2,1,0:T(1,128)} %bitcast.4), calls=%async_computation | async-start | bytes 278528 | tf_op jit(solution)/shard_map/all_to_all | solution.py:312
  10.5 0.0 copy-done.2
  10.5 1.6 %collective-permute-start = (f32[16,512]{1,0:T(8,128)S(1)}, f32[16,512]{1,0:T(8,128)S(1)}, u32[]{:S(2)}, u32[]{:S(2)}) collective-permute-start(f32[16,512]{1,0:T(8,128)S(1)} %copy-done.2), channel_id=1, source_target_pairs={{0,16},{16,0},{1,17},{17,1},{2,18},{18,2},{3,19},{19,3},{4,20},{20... | collective-permute-start | bytes 98312 | tf_op jit(solution)/shard_map/ppermute | solution.py:335
  12.1 0.0 collective-permute-done.1.inverse_ref
  12.1 0.3 %square.1 = (bf16[4,128,128]{2,1,0:T(8,128)(2,1)S(1)}, bf16[4,128,128]{2,1,0:T(8,128)(2,1)S(1)}) custom-call(f32[4,128,128]{2,1,0:T(8,128)S(1)} %collective-permute-done.1.inverse_ref), custom_call_target="tpu_custom_call" | custom-call | flops 20000000000 | tf_op jit(solution)/shard_map/square/pallas_call | solution.py:339
  12.4 0.0 copy-start
  12.4 1.3 %collective-permute-done.rhs_ref = f32[16,512]{1,0:T(8,128)S(1)} collective-permute-done((f32[16,512]{1,0:T(8,128)S(1)}, f32[16,512]{1,0:T(8,128)S(1)}, u32[]{:S(2)}, u32[]{:S(2)}) %collective-permute-start) | collective-permute-done | bytes 32800 | tf_op jit(solution)/shard_map/ppermute | solution.py:335
  13.7 1.2 %all-to-all-done = f32[16,17,1,128]{3,2,1,0:T(1,128)S(1)} async-done(((f32[16,17,1,128]{3,2,1,0:T(1,128)}), f32[16,17,1,128]{3,2,1,0:T(1,128)S(1)}, u32[]{:S(2)}, u32[]{:S(2)}) %all-to-all-start) | async-done | bytes 139296 | tf_op jit(solution)/shard_map/all_to_all | solution.py:312
  14.9 0.9 %last_section.1 = (f32[16,512]{1,0:T(8,128)S(1)}, f32[16,16,128]{2,1,0:T(8,128)}) custom-call(f32[272,128]{1,0:T(8,128)S(1)} %bitcast.3, f32[16,512]{1,0:T(8,128)S(1)} %collective-permute-done.rhs_ref, bf16[4,128,128]{2,1,0:T(8,128)(2,1)S(1)} %get-tuple-element.27.high_ref, bf16[4,128,128]{2,1,0:T(8,128)(2,1)S(1)} %get-tuple-element.28.low_ref), custom_call_target="tpu_custom_call" | custom-call | tf_op jit(solution)/shard_map/last_section/pallas_call | solution.py:350
  15.8 0.0 copy-start.3
  15.8 0.0 copy-start.4
  15.8 5.2 %all-to-all-start.1 = ((f32[16,16,128]{2,1,0:T(8,128)}), f32[16,16,128]{2,1,0:T(8,128)S(1)}, u32[]{:S(2)}, u32[]{:S(2)}) async-start(f32[16,16,128]{2,1,0:T(8,128)} %get-tuple-element.33), calls=%async_computation.1 | async-start | bytes 262144 | tf_op jit(solution)/shard_map/all_to_all | solution.py:312
  21.0 1.5 %collective-permute-start.2 = (f32[16,512]{1,0:T(8,128)S(1)}, f32[16,512]{1,0:T(8,128)S(1)}, u32[]{:S(2)}, u32[]{:S(2)}) collective-permute-start(f32[16,512]{1,0:T(8,128)S(1)} %get-tuple-element.29), channel_id=1, source_target_pairs={{0,16},{16,0},{1,17},{17,1},{2,18},{18,2},{3,19},{19,3},{4,20},{20... | collective-permute-start | bytes 98312 | tf_op jit(solution)/shard_map/ppermute | solution.py:374
  22.5 0.0 copy-done
  22.5 0.0 copy-done.3
  22.5 0.0 copy-done.4
  22.5 0.5 %fold.1 = (s32[8,128]{1,0:T(8,128)S(1)}, f32[16,512]{1,0:T(8,128)S(1)}, f32[16,512]{1,0:T(8,128)S(1)}, f32[16,512]{1,0:T(8,128)S(1)}, bf16[4,128,128]{2,1,0:T(8,...) custom-call(s32[8,128]{1,0:T(8,128)S(1)} %copy-done.4, ...), custom_call_target="tpu_custom_call" | custom-call | flops 20000000000 | tf_op jit(solution)/shard_map/fold/pallas_call | solution.py:342
  23.1 2.0 %all-to-all-done.1.picked_ref = f32[16,16,128]{2,1,0:T(8,128)S(1)} async-done(((f32[16,16,128]{2,1,0:T(8,128)}), f32[16,16,128]{2,1,0:T(8,128)S(1)}, u32[]{:S(2)}, u32[]{:S(2)}) %all-to-all-start.1) | async-done | bytes 131104 | tf_op jit(solution)/shard_map/all_to_all | solution.py:312
  25.0 1.0 %backward_last.1 = (f32[16,512]{1,0:T(8,128)}, f32[16,512]{1,0:T(8,128)}) custom-call(s32[8,128]{1,0:T(8,128)S(1)} %get-tuple-element.32.slots_ref, f32[16,16,128]{2,1,0:T(8,128)S(1)} %all-to-all-done.1.picked_ref, f32[16,512]{1,0:T(8,128)S(1)} %get-tuple-element.34.base_ref, bf16[4,2,128,128]{3,2,1,0:T(8,128)(2,1)S(1)} %get-tuple-element.35.high_ref, ...), custom_call_target="tpu_custom_call" | custom-call | tf_op jit(solution)/shard_map/backward_last/pallas_call | solution.py:366
  26.1 0.0 collective-permute-done.2.sums_ref
  (1 shorter events, 0.0 us)
Async XLA Ops:
  0.6 2.2 %copy-start.1 = (f32[4,128,128]{2,1,0:T(8,128)S(1)}, f32[4,128,128]{2,1,0:T(8,128)}, u32[]{:S(2)}) copy-start(f32[4,128,128]{2,1,0:T(8,128)} %inverse_ref.1) | copy-start | bytes 786436
  2.8 9.3 %collective-permute-start.1 = (f32[4,128,128]{2,1,0:T(8,128)S(1)}, f32[4,128,128]{2,1,0:T(8,128)S(1)}, u32[]{:S(2)}, u32[]{:S(2)}) collective-permute-start(f32[4,128,128]{2,1,0:T(8,128)S(1)} %copy-done.1), channel_id=1, source_target_pairs={{0,16},{16,0},{1,17},{17,1},{2,18},{18,2},{3,19},{19,3},{4,20},{20... | collective-permute-start | bytes 786440 | tf_op jit(solution)/shard_map/ppermute | solution.py:334
  3.7 6.8 %copy-start.2 = (f32[16,512]{1,0:T(8,128)S(1)}, f32[16,512]{1,0:T(8,128)}, u32[]{:S(2)}) copy-start(f32[16,512]{1,0:T(8,128)} %rhs_ref.1) | copy-start | bytes 98308
  3.7 11.2 %all-to-all-start = ((f32[16,17,1,128]{3,2,1,0:T(1,128)}), f32[16,17,1,128]{3,2,1,0:T(1,128)S(1)}, u32[]{:S(2)}, u32[]{:S(2)}) async-start(f32[16,17,1,128]{3,2,1,0:T(1,128)} %bitcast.4), calls=%async_computation | async-start | bytes 278528 | tf_op jit(solution)/shard_map/all_to_all | solution.py:312
  10.5 3.2 %collective-permute-start = (f32[16,512]{1,0:T(8,128)S(1)}, f32[16,512]{1,0:T(8,128)S(1)}, u32[]{:S(2)}, u32[]{:S(2)}) collective-permute-start(f32[16,512]{1,0:T(8,128)S(1)} %copy-done.2), channel_id=1, source_target_pairs={{0,16},{16,0},{1,17},{17,1},{2,18},{18,2},{3,19},{19,3},{4,20},{20... | collective-permute-start | bytes 98312 | tf_op jit(solution)/shard_map/ppermute | solution.py:335
  12.4 10.1 %copy-start = (f32[4,2,128,128]{3,2,1,0:T(8,128)S(1)}, f32[4,2,128,128]{3,2,1,0:T(8,128)}, u32[]{:S(2)}) copy-start(f32[4,2,128,128]{3,2,1,0:T(8,128)} %couplings_ref.1) | copy-start | bytes 1572868
  15.8 6.8 %copy-start.3 = (f32[16,512]{1,0:T(8,128)S(1)}, f32[16,512]{1,0:T(8,128)}, u32[]{:S(2)}) copy-start(f32[16,512]{1,0:T(8,128)} %get-tuple-element.22.values_ref) | copy-start | bytes 98308
  15.8 6.8 %copy-start.4 = (s32[8,128]{1,0:T(8,128)S(1)}, s32[8,128]{1,0:T(8,128)}, u32[]{:S(2)}) copy-start(s32[8,128]{1,0:T(8,128)} %get-tuple-element.21.slots_ref) | copy-start | bytes 12292
  15.8 9.3 %all-to-all-start.1 = ((f32[16,16,128]{2,1,0:T(8,128)}), f32[16,16,128]{2,1,0:T(8,128)S(1)}, u32[]{:S(2)}, u32[]{:S(2)}) async-start(f32[16,16,128]{2,1,0:T(8,128)} %get-tuple-element.33), calls=%async_computation.1 | async-start | bytes 262144 | tf_op jit(solution)/shard_map/all_to_all | solution.py:312
  21.0 5.1 %collective-permute-start.2 = (f32[16,512]{1,0:T(8,128)S(1)}, f32[16,512]{1,0:T(8,128)S(1)}, u32[]{:S(2)}, u32[]{:S(2)}) collective-permute-start(f32[16,512]{1,0:T(8,128)S(1)} %get-tuple-element.29), channel_id=1, source_target_pairs={{0,16},{16,0},{1,17},{17,1},{2,18},{18,2},{3,19},{19,3},{4,20},{20... | collective-permute-start | bytes 98312 | tf_op jit(solution)/shard_map/ppermute | solution.py:374

commit v7 on v6

--- a/solution.py
+++ b/solution.py
@@ -90,6 +90,8 @@
     base_ref,
     inverse_high_ref,
     inverse_low_ref,
+    square_high_ref,
+    square_low_ref,
     high_ref,
     low_ref,
 ):
@@ -101,6 +103,7 @@
         inverse = inverse_ref[local]
         parts = split(inverse)
         inverse_high_ref[local], inverse_low_ref[local] = parts
+        square_high_ref[local], square_low_ref[local] = split(times_transposed(inverse, parts))
         base_ref[:, lanes] = times_transposed(values_ref[:, lanes], parts)
         for k in range(fanout):
             product = times(inverse, split(couplings_ref[local, k]))
@@ -196,14 +199,6 @@
         sums_ref[:, lanes[local]] = total
 
 
-def solve_last(rhs_ref, sums, high_ref, low_ref):
-    local_count, width, _ = high_ref.shape
-    lanes = lane_blocks(width, local_count)
-    inverse = [(high_ref[i], low_ref[i]) for i in range(local_count)]
-    forward = [times(rhs_ref[:, lanes[i]] - sums[i], inverse[i]) for i in range(local_count)]
-    return forward, [times_transposed(forward[i], inverse[i]) for i in range(local_count)]
-
-
 def last_kernel(arrived_ref, rhs_ref, high_ref, low_ref, sums_ref, *rest):
     *solved_ref, answers_ref = rest
     local_count, width, _ = high_ref.shape
@@ -264,25 +259,27 @@
         second.wait()
 
 
-def finish_kernel(rhs_ref, sums_ref, high_ref, low_ref, *rest):
-    _, _, forward_out, solution_out, forward_ref, solution_ref, sems = rest
+def finish_kernel(rhs_ref, sums_ref, *rest):
+    weights, (forward_out, solution_out, forward_ref, solution_ref, sems) = rest[:4], rest[6:]
+    high_ref, low_ref, square_high_ref, square_low_ref = weights
     section_is_last = lax.axis_index("section") == lax.axis_size("section") - 1
 
     @pl.when(section_is_last)
     def _():
-        local_count, width, _ = high_ref.shape
-        lanes = lane_blocks(width, local_count)
-        sums = [sums_ref[:, lane] for lane in lanes]
-        forward, backward = solve_last(rhs_ref, sums, high_ref, low_ref)
-        for local, lane in enumerate(lanes):
-            forward_ref[:, lane] = forward[local]
-            solution_ref[:, lane] = backward[local]
         copies = [
             pltpu.make_async_copy(forward_ref, forward_out, sems.at[0]),
             pltpu.make_async_copy(solution_ref, solution_out, sems.at[1]),
         ]
-        for copy in copies:
-            copy.start()
+        local_count, width, _ = high_ref.shape
+        lanes = lane_blocks(width, local_count)
+        sources = [rhs_ref[:, lane] - sums_ref[:, lane] for lane in lanes]
+        for local, lane in enumerate(lanes):
+            forward_ref[:, lane] = times(sources[local], (high_ref[local], low_ref[local]))
+        copies[0].start()
+        for local, lane in enumerate(lanes):
+            square = (square_high_ref[local], square_low_ref[local])
+            solution_ref[:, lane] = times(sources[local], square)
+        copies[1].start()
         for copy in copies:
             copy.wait()
 
@@ -339,9 +336,9 @@
     next_square = kernel_call(square_kernel, halves(inverse_blocks), [VMEM], "square", COVER)(
         next_inverse
     )
-    slot_rows, values, own_rhs, base, *own_inverse, high, low = kernel_call(
+    slot_rows, values, own_rhs, base, *own_weights, high, low = kernel_call(
         fold_kernel,
-        (owners, flat, flat, flat, *halves(inverse_blocks), *halves(couplings)),
+        (owners, flat, flat, flat, *halves(inverse_blocks) * 2, *halves(couplings)),
         [VMEM] * 5,
         "fold",
         COVER,
@@ -375,12 +372,12 @@
     return kernel_call(
         finish_kernel,
         (flat, flat),
-        [VMEM] * 4 + [HBM] * 2,
+        [VMEM] * 6 + [HBM] * 2,
         "finish_last",
         scratch=[staged, staged, sems],
         out_specs=(HBM, HBM),
-        aliases={4: 0, 5: 1},
-    )(own_rhs, received, *own_inverse, *results)
+        aliases={6: 0, 7: 1},
+    )(own_rhs, received, *own_weights, *results)
 
 
 def solution(mesh):

time: 26.5 us -> 26.5 us (level)
  no operation moved by 1% of the time
where the time goes in v7:
time: 26.5 us; the launch traced here: 26.1 us
  starting transfers between devices  16 us (60%)
  Pallas kernels  5.04 us (19%)
  waiting for transfers between devices  4.35 us (16%)
  between operations  0.7 us (3%)
    all_to_all x2, starting transfers between devices, exchanged(): lax.all_to_all(value, 'col', split_axis=0, concat_axis=0, tiled=True, axi...  12 us
    all_to_all x2, waiting for transfers between devices, exchanged(): lax.all_to_all(value, 'col', split_axis=0, concat_axis=0, tiled=True, axi...  3.07 us
    pallas_call x1, Pallas kernels, body(): kernel_call(forward_kernel, (flat, owners, slots), [HBM] * len(inputs) +...  2.18 us
    ppermute x1, starting transfers between devices, body(): next_rhs = lax.ppermute(sent_rhs, 'section', down)  1.6 us
    ppermute x1, starting transfers between devices, body(): received = lax.ppermute(sums, 'section', up)  1.53 us
    ppermute x1, waiting for transfers between devices, body(): next_rhs = lax.ppermute(sent_rhs, 'section', down)  1.28 us
    pallas_call x1, Pallas kernels, body(): kernel_call(backward_kernel, (flat, flat), [VMEM] * (len(operands) + 1),...  1.02 us
    pallas_call x1, Pallas kernels, body(): kernel_call(last_kernel, last_shapes, [VMEM] * 4, 'last_section')  0.88 us
  transfers between devices with their start and end apart: 5, of which 3 were waited for; matrix products, arithmetic and copies ran while one was open for 0% of the time, Pallas kernels for 7%

profile of v7, /device:TPU:1, one launch (start us, length us, event | category | flops | bytes accessed | tf_op | source)
XLA Modules:
  0.0 26.1 jit_solution(12965506091428737614)
XLA Ops:
  0.6 0.0 copy-start.1
  0.6 2.2 %forward.1 = (f32[16,512]{1,0:T(8,128)}, s32[8,128]{1,0:T(8,128)}, f32[272,128]{1,0:T(8,128)}) custom-call(s32[2,4]{1,0:T(2,128)} %bitcast.5, f32[16,512]{1,0:T(8,128)} %rhs_ref.1, f32[4,128,128]{2,1,0:T(8,128)} %inverse_ref.1, f32[4,2,128,128]{3,2,1,0:T(8,128)} %couplings_ref.1), custom_call_target="tpu_custom_call" | custom-call | tf_op jit(solution)/shard_map/forward/pallas_call | solution.py:315
  2.8 0.0 copy-done.1
  2.8 0.8 %collective-permute-start.1 = (f32[4,128,128]{2,1,0:T(8,128)S(1)}, f32[4,128,128]{2,1,0:T(8,128)S(1)}, u32[]{:S(2)}, u32[]{:S(2)}) collective-permute-start(f32[4,128,128]{2,1,0:T(8,128)S(1)} %copy-done.1), channel_id=1, source_target_pairs={{0,16},{16,0},{1,17},{17,1},{2,18},{18,2},{3,19},{19,3},{4,20},{20... | collective-permute-start | bytes 786440 | tf_op jit(solution)/shard_map/ppermute | solution.py:331
  3.7 0.0 copy-start.2
  3.7 6.8 %all-to-all-start = ((f32[16,17,1,128]{3,2,1,0:T(1,128)}), f32[16,17,1,128]{3,2,1,0:T(1,128)S(1)}, u32[]{:S(2)}, u32[]{:S(2)}) async-start(f32[16,17,1,128]{3,2,1,0:T(1,128)} %bitcast.4), calls=%async_computation | async-start | bytes 278528 | tf_op jit(solution)/shard_map/all_to_all | solution.py:309
  10.5 0.0 copy-done.2
  10.5 1.6 %collective-permute-start = (f32[16,512]{1,0:T(8,128)S(1)}, f32[16,512]{1,0:T(8,128)S(1)}, u32[]{:S(2)}, u32[]{:S(2)}) collective-permute-start(f32[16,512]{1,0:T(8,128)S(1)} %copy-done.2), channel_id=1, source_target_pairs={{0,16},{16,0},{1,17},{17,1},{2,18},{18,2},{3,19},{19,3},{4,20},{20... | collective-permute-start | bytes 98312 | tf_op jit(solution)/shard_map/ppermute | solution.py:332
  12.1 0.0 collective-permute-done.1.inverse_ref
  12.1 0.3 %square.1 = (bf16[4,128,128]{2,1,0:T(8,128)(2,1)S(1)}, bf16[4,128,128]{2,1,0:T(8,128)(2,1)S(1)}) custom-call(f32[4,128,128]{2,1,0:T(8,128)S(1)} %collective-permute-done.1.inverse_ref), custom_call_target="tpu_custom_call" | custom-call | flops 20000000000 | tf_op jit(solution)/shard_map/square/pallas_call | solution.py:336
  12.4 0.0 copy-start
  12.4 1.3 %collective-permute-done.rhs_ref = f32[16,512]{1,0:T(8,128)S(1)} collective-permute-done((f32[16,512]{1,0:T(8,128)S(1)}, f32[16,512]{1,0:T(8,128)S(1)}, u32[]{:S(2)}, u32[]{:S(2)}) %collective-permute-start) | collective-permute-done | bytes 32800 | tf_op jit(solution)/shard_map/ppermute | solution.py:332
  13.7 1.2 %all-to-all-done = f32[16,17,1,128]{3,2,1,0:T(1,128)S(1)} async-done(((f32[16,17,1,128]{3,2,1,0:T(1,128)}), f32[16,17,1,128]{3,2,1,0:T(1,128)S(1)}, u32[]{:S(2)}, u32[]{:S(2)}) %all-to-all-start) | async-done | bytes 139296 | tf_op jit(solution)/shard_map/all_to_all | solution.py:309
  14.9 0.9 %last_section.1 = (f32[16,512]{1,0:T(8,128)S(1)}, f32[16,16,128]{2,1,0:T(8,128)}) custom-call(f32[272,128]{1,0:T(8,128)S(1)} %bitcast.3, f32[16,512]{1,0:T(8,128)S(1)} %collective-permute-done.rhs_ref, bf16[4,128,128]{2,1,0:T(8,128)(2,1)S(1)} %get-tuple-element.29.high_ref, bf16[4,128,128]{2,1,0:T(8,128)(2,1)S(1)} %get-tuple-element.30.low_ref), custom_call_target="tpu_custom_call" | custom-call | tf_op jit(solution)/shard_map/last_section/pallas_call | solution.py:347
  15.8 0.0 copy-start.3
  15.8 0.0 copy-start.4
  15.8 5.2 %all-to-all-start.1 = ((f32[16,16,128]{2,1,0:T(8,128)}), f32[16,16,128]{2,1,0:T(8,128)S(1)}, u32[]{:S(2)}, u32[]{:S(2)}) async-start(f32[16,16,128]{2,1,0:T(8,128)} %get-tuple-element.37), calls=%async_computation.1 | async-start | bytes 262144 | tf_op jit(solution)/shard_map/all_to_all | solution.py:309
  21.0 1.5 %collective-permute-start.2 = (f32[16,512]{1,0:T(8,128)S(1)}, f32[16,512]{1,0:T(8,128)S(1)}, u32[]{:S(2)}, u32[]{:S(2)}) collective-permute-start(f32[16,512]{1,0:T(8,128)S(1)} %get-tuple-element.31), channel_id=1, source_target_pairs={{0,16},{16,0},{1,17},{17,1},{2,18},{18,2},{3,19},{19,3},{4,20},{20... | collective-permute-start | bytes 98312 | tf_op jit(solution)/shard_map/ppermute | solution.py:371
  22.5 0.0 copy-done
  22.5 0.0 copy-done.3
  22.5 0.0 copy-done.4
  22.5 0.6 %fold.1 = (s32[8,128]{1,0:T(8,128)S(1)}, f32[16,512]{1,0:T(8,128)S(1)}, f32[16,512]{1,0:T(8,128)S(1)}, f32[16,512]{1,0:T(8,128)S(1)}, bf16[4,128,128]{2,1,0:T(8,...) custom-call(s32[8,128]{1,0:T(8,128)S(1)} %copy-done.4, ...), custom_call_target="tpu_custom_call" | custom-call | flops 20000000000 | tf_op jit(solution)/shard_map/fold/pallas_call | solution.py:339
  23.1 1.9 %all-to-all-done.1.picked_ref = f32[16,16,128]{2,1,0:T(8,128)S(1)} async-done(((f32[16,16,128]{2,1,0:T(8,128)}), f32[16,16,128]{2,1,0:T(8,128)S(1)}, u32[]{:S(2)}, u32[]{:S(2)}) %all-to-all-start.1) | async-done | bytes 131104 | tf_op jit(solution)/shard_map/all_to_all | solution.py:309
  25.0 1.0 %backward_last.1 = (f32[16,512]{1,0:T(8,128)}, f32[16,512]{1,0:T(8,128)}) custom-call(s32[8,128]{1,0:T(8,128)S(1)} %get-tuple-element.36.slots_ref, f32[16,16,128]{2,1,0:T(8,128)S(1)} %all-to-all-done.1.picked_ref, f32[16,512]{1,0:T(8,128)S(1)} %get-tuple-element.38.base_ref, bf16[4,2,128,128]{3,2,1,0:T(8,128)(2,1)S(1)} %get-tuple-element.39.high_ref, ...), custom_call_target="tpu_custom_call" | custom-call | tf_op jit(solution)/shard_map/backward_last/pallas_call | solution.py:363
  26.1 0.0 collective-permute-done.2.sums_ref
  (1 shorter events, 0.0 us)
Async XLA Ops:
  0.6 2.2 %copy-start.1 = (f32[4,128,128]{2,1,0:T(8,128)S(1)}, f32[4,128,128]{2,1,0:T(8,128)}, u32[]{:S(2)}) copy-start(f32[4,128,128]{2,1,0:T(8,128)} %inverse_ref.1) | copy-start | bytes 786436
  2.8 9.3 %collective-permute-start.1 = (f32[4,128,128]{2,1,0:T(8,128)S(1)}, f32[4,128,128]{2,1,0:T(8,128)S(1)}, u32[]{:S(2)}, u32[]{:S(2)}) collective-permute-start(f32[4,128,128]{2,1,0:T(8,128)S(1)} %copy-done.1), channel_id=1, source_target_pairs={{0,16},{16,0},{1,17},{17,1},{2,18},{18,2},{3,19},{19,3},{4,20},{20... | collective-permute-start | bytes 786440 | tf_op jit(solution)/shard_map/ppermute | solution.py:331
  3.7 6.8 %copy-start.2 = (f32[16,512]{1,0:T(8,128)S(1)}, f32[16,512]{1,0:T(8,128)}, u32[]{:S(2)}) copy-start(f32[16,512]{1,0:T(8,128)} %rhs_ref.1) | copy-start | bytes 98308
  3.7 11.2 %all-to-all-start = ((f32[16,17,1,128]{3,2,1,0:T(1,128)}), f32[16,17,1,128]{3,2,1,0:T(1,128)S(1)}, u32[]{:S(2)}, u32[]{:S(2)}) async-start(f32[16,17,1,128]{3,2,1,0:T(1,128)} %bitcast.4), calls=%async_computation | async-start | bytes 278528 | tf_op jit(solution)/shard_map/all_to_all | solution.py:309
  10.5 3.2 %collective-permute-start = (f32[16,512]{1,0:T(8,128)S(1)}, f32[16,512]{1,0:T(8,128)S(1)}, u32[]{:S(2)}, u32[]{:S(2)}) collective-permute-start(f32[16,512]{1,0:T(8,128)S(1)} %copy-done.2), channel_id=1, source_target_pairs={{0,16},{16,0},{1,17},{17,1},{2,18},{18,2},{3,19},{19,3},{4,20},{20... | collective-permute-start | bytes 98312 | tf_op jit(solution)/shard_map/ppermute | solution.py:332
  12.4 10.1 %copy-start = (f32[4,2,128,128]{3,2,1,0:T(8,128)S(1)}, f32[4,2,128,128]{3,2,1,0:T(8,128)}, u32[]{:S(2)}) copy-start(f32[4,2,128,128]{3,2,1,0:T(8,128)} %couplings_ref.1) | copy-start | bytes 1572868
  15.8 6.8 %copy-start.3 = (f32[16,512]{1,0:T(8,128)S(1)}, f32[16,512]{1,0:T(8,128)}, u32[]{:S(2)}) copy-start(f32[16,512]{1,0:T(8,128)} %get-tuple-element.24.values_ref) | copy-start | bytes 98308
  15.8 6.8 %copy-start.4 = (s32[8,128]{1,0:T(8,128)S(1)}, s32[8,128]{1,0:T(8,128)}, u32[]{:S(2)}) copy-start(s32[8,128]{1,0:T(8,128)} %get-tuple-element.23.slots_ref) | copy-start | bytes 12292
  15.8 9.3 %all-to-all-start.1 = ((f32[16,16,128]{2,1,0:T(8,128)}), f32[16,16,128]{2,1,0:T(8,128)S(1)}, u32[]{:S(2)}, u32[]{:S(2)}) async-start(f32[16,16,128]{2,1,0:T(8,128)} %get-tuple-element.37), calls=%async_computation.1 | async-start | bytes 262144 | tf_op jit(solution)/shard_map/all_to_all | solution.py:309
  21.0 5.1 %collective-permute-start.2 = (f32[16,512]{1,0:T(8,128)S(1)}, f32[16,512]{1,0:T(8,128)S(1)}, u32[]{:S(2)}, u32[]{:S(2)}) collective-permute-start(f32[16,512]{1,0:T(8,128)S(1)} %get-tuple-element.31), channel_id=1, source_target_pairs={{0,16},{16,0},{1,17},{17,1},{2,18},{18,2},{3,19},{19,3},{4,20},{20... | collective-permute-start | bytes 98312 | tf_op jit(solution)/shard_map/ppermute | solution.py:371
